TPU v7x, 128 devices: a whole 4x4x4 slice. The times are simulated.
128 devices in a mesh: blk: 16 (over x, y_hi, core), head: 8 (over y_lo, z).
Axes of the slice: x: 4, y: 4 (y_hi: 2, y_lo: 2; y = y_hi * 2 + y_lo), z: 4, core: 2. Of those that a mesh axis runs over, the one named last changes fastest.
Arguments:
- queries: bfloat16 [16384, 3072], P(('blk', 'head')), may hold values from -8 to 8
- keys: bfloat16 [16384, 3072], P(('blk', 'head')), may hold values from -8 to 8
- values: bfloat16 [16384, 3072], P(('blk', 'head')), may hold values from -6 to 6
- d_queries: bfloat16 [16384, 3072], P(('blk', 'head')), may hold values from -6 to 6
- d_keys: bfloat16 [16384, 3072], P(('blk', 'head')), may hold values from -6 to 6
- d_values: bfloat16 [16384, 3072], P(('blk', 'head')), may hold values from -6 to 6
- positions: int32 [3, 16384], P(None, ('blk', 'head')), may hold values from 0 to 79, as said below
- key_lists: int32 [16, 5], replicated, may hold values from -1 to 15, as said below
Outputs:
- attended: bfloat16 [16384, 3072], P(('blk', 'head'))
- d_attended: bfloat16 [16384, 3072], P(('blk', 'head'))
Inputs may be any that keep to these rules, and one draw needn't show every extreme that they name: `key_lists`: row r lists between 1 and 5 different key blocks, each within 3 of r, always r itself, nearer blocks more often; unused slots are -1 and come last; some row lists exactly 5 blocks. `positions`: frame indices are below 21, height indices below 45, width indices below 80.
All inputs are finite; a program needn't handle non-finite values.
Results may differ from a plain program's by a relative error of at most 0.018.
Values may be sent and summed in bfloat16 or wider, within the bound.
A program may use at most 192 MiB of HBM per device.

v0:
```python
import functools

import jax
import jax.numpy as jnp
import numpy as np
from jax import lax
from jax.experimental import pallas as pl
from jax.experimental.pallas import tpu as pltpu
from jax.sharding import PartitionSpec as P

MESH = pl.DeviceIdType.MESH
REACH = 3
BLOCKS = 16
CHUNK = 128
QB = 1024
SCALE = 128 ** (-0.5)
LOG2E = 1.4426950408889634
CHIP_X = (0, 2, 3, 1, 2, 0, 1, 3)
SLOTS = 12
ORDER = (0, 5, 2, 3, 1, 4)


def chip_runs():
    runs = []
    for k in range(8):
        mine, base = [], 0
        for j in range(3):
            blocks = [job % 16 for job in range(6 * k, 6 * k + 6) if job // 16 == j]
            if blocks:
                low, high = max(0, blocks[0] - REACH), min(BLOCKS - 1, blocks[-1] + REACH)
                mine.append((j, low, high, base))
                base += high - low + 1
        runs.append(mine)
    return runs


RUNS = chip_runs()
CHIP_AT = [[CHIP_X[4 * side : 4 * side + 4].index(x) + 4 * side for x in range(4)] for side in range(2)]


def pick(index, values):
    result = jnp.int32(values[0])
    for place, value in enumerate(values[1:], 1):
        if value != values[0]:
            result = jnp.where(index == place, jnp.int32(value), result)
    return result


def run_code(k, j):
    for head, low, high, base in RUNS[k]:
        if head == j:
            return (low * 64 + high) * 64 + base
    return (63 * 64) * 64


def coordinates():
    block = lax.axis_index("blk")
    part = lax.axis_index("head")
    x, y_hi, core = block // 4, (block // 2) % 2, block % 2
    y_lo, z = part // 4, part % 4
    return block, x, y_hi, y_lo, 2 * y_hi + y_lo, z, core


def device(x, y, z, core):
    return (4 * x + 2 * (y // 2) + core, 4 * (y % 2) + z)


def my_chip(x, y):
    return pick(4 * (y % 2) + x, CHIP_AT[0] + CHIP_AT[1])


def frequency_rows():
    tables = np.zeros((3, 128), np.float32)
    start = 0
    for axis_id, count, span in ((0, 22, 44), (1, 21, 42), (2, 21, 42)):
        for column in range(count):
            rate = 1.0 / 10000.0 ** (2.0 * column / span)
            tables[axis_id, 2 * (start + column)] = rate
            tables[axis_id, 2 * (start + column) + 1] = rate
        start += count
    return tables


def swap_table():
    table = np.zeros((128, 128), np.float32)
    for pair in range(64):
        table[2 * pair + 1, 2 * pair] = -1.0
        table[2 * pair, 2 * pair + 1] = 1.0
    return table


def rotate_kernel(
    lists_ref, spots_ref, rates_ref, swap_ref, q_ref, k_ref, v_ref, dq_ref, dk_ref, dv_ref,
    kv_ref, qq_ref, table_ref, cos_ref, sin_ref,
):
    heads = kv_ref.shape[0]

    @pl.when(pl.program_id(0) == 0)
    def _():
        spots = spots_ref[...].astype(jnp.float32)
        angle = jnp.zeros((CHUNK, 128), jnp.float32)
        for axis_id in range(3):
            column = jnp.broadcast_to(spots[axis_id : axis_id + 1, :], (128, CHUNK)).T
            angle = angle + column * rates_ref[axis_id : axis_id + 1, :]
        cos_ref[...] = jnp.cos(angle)
        sin_ref[...] = jnp.sin(angle)
        _, x, _, _, y, _, core = coordinates()
        chip = my_chip(x, y)
        for i in range(3):
            job = 6 * chip + 2 * i + core
            j, block = job // 16, job % 16
            code = pick(3 * chip + j, [run_code(k, h) for k in range(8) for h in range(3)])
            low, base = code // 4096, code % 64
            last = jnp.int32(0)
            for s in range(5):
                entry = lists_ref[block, s]
                listed = entry >= 0
                last = jnp.where(listed, entry - low + base, last)
                table_ref[i, s] = last
                table_ref[3 + i, s] = listed.astype(jnp.int32)

    cosine, sine, swap = cos_ref[...], sin_ref[...], swap_ref[...]

    def turned(ref, lanes):
        part = ref[:, lanes]
        swapped = jnp.dot(part, swap, preferred_element_type=jnp.float32)
        return (part.astype(jnp.float32) * cosine + swapped * sine).astype(jnp.bfloat16)

    for head in range(heads):
        lanes = slice(128 * head, 128 * head + 128)
        kv_ref[head, :, 0:128] = turned(k_ref, lanes)
        kv_ref[head, :, 128:256] = turned(dk_ref, lanes)
        kv_ref[head, :, 256:384] = v_ref[:, lanes]
        kv_ref[head, :, 384:512] = dv_ref[:, lanes]
        qq_ref[head, :, 0:128] = turned(dq_ref, lanes)
        qq_ref[head, :, 128:256] = turned(q_ref, lanes)


def rotate_all(queries, keys, values, d_queries, d_keys, d_values, positions, key_lists):
    group = 4
    steps = 24 // group
    whole = pl.BlockSpec(memory_space=pltpu.VMEM)
    columns = pl.BlockSpec((CHUNK, 128 * group), lambda i: (0, i))
    return pl.pallas_call(
        rotate_kernel,
        name="rotate",
        grid=(steps,),
        out_shape=(
            jax.ShapeDtypeStruct((24, CHUNK, 512), jnp.bfloat16),
            jax.ShapeDtypeStruct((24, CHUNK, 256), jnp.bfloat16),
            jax.ShapeDtypeStruct((6, 5), jnp.int32),
        ),
        in_specs=[pl.BlockSpec(memory_space=pltpu.SMEM), whole, whole, whole] + [columns] * 6,
        out_specs=(
            pl.BlockSpec((group, CHUNK, 512), lambda i: (i, 0, 0)),
            pl.BlockSpec((group, CHUNK, 256), lambda i: (i, 0, 0)),
            pl.BlockSpec(memory_space=pltpu.SMEM),
        ),
        scratch_shapes=[pltpu.VMEM((CHUNK, 128), jnp.float32)] * 2,
        compiler_params=pltpu.CompilerParams(vmem_limit_bytes=32 * 2**20),
    )(
        key_lists, positions, jnp.asarray(frequency_rows()), jnp.asarray(swap_table(), jnp.bfloat16),
        queries, keys, values, d_queries, d_keys, d_values,
    )


def bring_kernel(
    pkv, pq, zkv, zq, ykv, yq, kv, qq,
    zs, zqs, ys, yqs, xs, xqs, fs, zr, zqr, yr, yqr, kr, qr, fr,
):
    block, x, y_hi, y_lo, y, z, core = coordinates()
    side = y % 2
    chip = my_chip(x, y)

    barrier = pltpu.get_barrier_semaphore()
    partners = (
        [device(x, y, (z + d) % 4, core) for d in (1, 2, 3)]
        + [device(x, (y + d) % 4, z, core) for d in (1, 2, 3)]
        + [device((x + d) % 4, y, z, core) for d in (1, 2, 3)]
        + [device(x, y, z, 1 - core)]
    )
    for partner in partners:
        pl.semaphore_signal(barrier, inc=1, device_id=partner, device_id_type=MESH)
    pl.semaphore_wait(barrier, len(partners))

    sent = []

    def send(where, here, source, target, send_sem, recv_sem, to):
        if here is not False:

            @pl.when(jnp.logical_and(where, here))
            def _():
                pltpu.make_async_copy(source, target, recv_sem).start()

        if here is not True:
            away = where if here is False else jnp.logical_and(where, jnp.logical_not(here))
            remote = pltpu.make_async_remote_copy(
                src_ref=source, dst_ref=target, send_sem=send_sem, recv_sem=recv_sem, device_id=to, device_id_type=MESH
            )

            @pl.when(away)
            def _():
                remote.start()

            sent.append((away, remote))

    def arrived(where, target, recv_sem):
        @pl.when(where)
        def _():
            pltpu.make_async_copy(target, target, recv_sem).wait()

    always = block >= 0
    rows_z = pl.ds(pl.multiple_of(z * CHUNK, CHUNK), CHUNK)
    for hh in ORDER:
        for d in (2, 1, 3, 0):
            to = (z + d) % 4
            head = 6 * to + hh
            place = device(x, y, to, core)
            send(always, d == 0, pkv.at[head], zkv.at[hh, rows_z], zs.at[hh, d], zr.at[hh], place)
            send(always, d == 0, pq.at[head], zq.at[hh, rows_z], zqs.at[hh, d], zqr.at[hh], place)

    rows_y = pl.ds(pl.multiple_of(y_lo * 512, 512), 512)

    def step_y(hh):
        g, j = hh // 3, hh % 3
        full = 1 if j == 1 else 0
        arrived(always, zkv.at[hh], zr.at[hh])
        for s in (0, 1):
            if (j, s) in ((0, 1), (2, 0)):
                continue
            where = always if j != 1 else (block <= 10 if s == 0 else block >= 5)
            to = 2 * g + s
            send(
                where, y == to, zkv.at[hh], ykv.at[full, y_hi, rows_y], ys.at[hh, s], yr.at[full, y_hi, y_lo],
                device(x, to, z, core),
            )
        arrived(always, zq.at[hh], zqr.at[hh])
        to = 2 * g + (16 * j + block) // 24
        send(
            always, y == to, zq.at[hh], yq.at[full, y_hi, rows_y], yqs.at[hh], yqr.at[full, y_hi],
            device(x, to, z, core),
        )

    def step_x(full):
        j = 1 if full else 2 * side
        for t in (0, 1):
            here = 4 * x + 2 * t + core
            came = always if full == 0 else jnp.logical_or(
                jnp.logical_and(side == 0, here <= 10), jnp.logical_and(side == 1, here >= 5)
            )
            for half in (0, 1):
                rows = pl.ds(512 * half, 512)
                arrived(came, ykv.at[full, t, rows], yr.at[full, t, half])
                for d in (2, 1, 3, 0):
                    to = (x + d) % 4
                    code = pick(
                        4 * side + to,
                        [run_code(CHIP_AT[s][xx], 1 if full else 2 * s) for s in range(2) for xx in range(4)],
                    )
                    low, high, base = code // 4096, (code // 64) % 64, code % 64
                    wanted = jnp.logical_and(here >= low, here <= high)
                    slot = jnp.where(wanted, here - low + base, 0)
                    send(
                        wanted, d == 0, ykv.at[full, t, rows], kv.at[slot, rows], xs.at[full, t, half, d], kr.at[slot],
                        device(to, y, z, core),
                    )
            job = 16 * j + here
            owned = job // 24 == side
            arrived(owned, yq.at[full, t], yqr.at[full, t])
            owner = job // 6
            to = pick(owner, CHIP_X)
            place = (job % 6) // 2
            send(
                owned, x == to, yq.at[full, t], qq.at[place], xqs.at[full, t], qr.at[place],
                device(to, y, z, core),
            )

    for hh in ORDER[:4]:
        step_y(hh)
    step_x(0)
    for hh in ORDER[4:]:
        step_y(hh)
    step_x(1)

    first = pick(chip, [RUNS[k][0][1] for k in range(8)])
    count = pick(chip, [sum(r[2] - r[1] + 1 for r in RUNS[k]) for k in range(8)])
    second = pick(chip, [RUNS[k][1][3] if len(RUNS[k]) > 1 else 63 for k in range(8)])
    second_low = pick(chip, [RUNS[k][1][1] if len(RUNS[k]) > 1 else 0 for k in range(8)])

    def slot_here(s):
        held = jnp.where(s < second, first + s, second_low + s - second)
        return s < count, held % 2 == core

    for s in range(SLOTS):
        used, mine = slot_here(s)
        direct = jnp.logical_and(used, mine)
        arrived(direct, kv.at[s], kr.at[s])
        send(direct, False, kv.at[s], kv.at[s], fs.at[s], fr.at[s], device(x, y, z, 1 - core))
    for s in range(SLOTS):
        used, mine = slot_here(s)
        arrived(jnp.logical_and(used, jnp.logical_not(mine)), kv.at[s], fr.at[s])
    for i in range(3):
        arrived(always, qq.at[i], qr.at[i])
    for away, remote in sent:

        @pl.when(away)
        def _():
            remote.wait_send()


def bring(pkv, pq):
    anywhere = pl.BlockSpec(memory_space=pl.ANY)
    dma = pltpu.SemaphoreType.DMA
    shapes = [
        (6, 512, 512), (6, 512, 256), (2, 2, QB, 512), (2, 2, QB, 256), (SLOTS, QB, 512), (3, QB, 256),
    ]
    sems = [
        (6, 4), (6, 4), (6, 2), (6,), (2, 2, 2, 4), (2, 2), (SLOTS,),
        (6,), (6,), (2, 2, 2), (2, 2), (SLOTS,), (3,), (SLOTS,),
    ]
    return pl.pallas_call(
        bring_kernel,
        name="bring",
        out_shape=tuple(jax.ShapeDtypeStruct(shape, jnp.bfloat16) for shape in shapes),
        in_specs=[anywhere] * 2,
        out_specs=(anywhere,) * len(shapes),
        scratch_shapes=[dma(shape) for shape in sems],
        compiler_params=pltpu.CompilerParams(collective_id=0, has_side_effects=True),
    )(pkv, pq)[4:]


def attend_kernel(table_ref, q_ref, kv_ref, out_ref, d_out_ref, top_ref, total_ref, light_ref, tilt_ref, rows=256):
    i, s = pl.program_id(0), pl.program_id(1)
    factor = SCALE * LOG2E

    @pl.when(s == 0)
    def _():
        top_ref[...] = jnp.full_like(top_ref, -jnp.inf)
        total_ref[...] = jnp.zeros_like(total_ref)
        light_ref[...] = jnp.zeros_like(light_ref)
        tilt_ref[...] = jnp.zeros_like(tilt_ref)

    @pl.when(table_ref[3 + i, s] == 1)
    def _():
        both_keys = kv_ref[0, :, 0:256]
        keys = kv_ref[0, :, 0:128]
        both_values = kv_ref[0, :, 256:512]
        ones = jnp.ones((QB, 128), jnp.bfloat16)
        values = jnp.concatenate([kv_ref[0, :, 256:384], ones], axis=1)
        across = (((1,), (1,)), ((), ()))

        for part in range(QB // rows):
            at = pl.ds(part * rows, rows)
            score = lax.dot_general(q_ref[0, at, 128:256], keys, across, preferred_element_type=jnp.float32)
            d_score = lax.dot_general(q_ref[0, at, :], both_keys, across, preferred_element_type=jnp.float32)
            old = top_ref[at, :]
            new = jnp.maximum(old, jnp.max(score, axis=1, keepdims=True))
            top_ref[at, :] = new
            fade = jnp.exp2((old - new) * factor)
            weight = jnp.exp2((score - new[:, 0:1]) * factor)
            tilted = weight * d_score
            partial = weight[:, 0:128]
            for c in range(1, QB // 128):
                partial = partial + weight[:, 128 * c : 128 * c + 128]
            total_ref[at, :] = total_ref[at, :] * fade + partial
            fade2 = jnp.concatenate([fade, fade], axis=1)
            light_ref[at, :] = light_ref[at, :] * fade2 + jnp.dot(
                weight.astype(jnp.bfloat16), both_values, preferred_element_type=jnp.float32
            )
            tilt_ref[at, :] = tilt_ref[at, :] * fade2 + jnp.dot(
                tilted.astype(jnp.bfloat16), values, preferred_element_type=jnp.float32
            )

    @pl.when(s == pl.num_programs(1) - 1)
    def _():
        inverse = 1.0 / jnp.sum(total_ref[...], axis=1, keepdims=True)
        out = light_ref[:, 0:128] * inverse
        moved = light_ref[:, 128:256] + SCALE * tilt_ref[:, 0:128]
        slope = SCALE * tilt_ref[:, 128:256]
        out_ref[0] = out.astype(jnp.bfloat16)
        d_out_ref[0] = (moved * inverse - slope * inverse * out).astype(jnp.bfloat16)


def attend(table, qq, kv):
    out = pl.BlockSpec((1, QB, 128), lambda i, s, table: (i, 0, 0))
    return pl.pallas_call(
        attend_kernel,
        name="attend",
        grid_spec=pltpu.PrefetchScalarGridSpec(
            num_scalar_prefetch=1,
            grid=(3, 5),
            in_specs=[
                pl.BlockSpec((1, QB, 256), lambda i, s, table: (i, 0, 0)),
                pl.BlockSpec((1, QB, 512), lambda i, s, table: (table[i, s], 0, 0)),
            ],
            out_specs=(out, out),
            scratch_shapes=[
                pltpu.VMEM((QB, 128), jnp.float32),
                pltpu.VMEM((QB, 128), jnp.float32),
                pltpu.VMEM((QB, 256), jnp.float32),
                pltpu.VMEM((QB, 256), jnp.float32),
            ],
        ),
        out_shape=(jax.ShapeDtypeStruct((3, QB, 128), jnp.bfloat16),) * 2,
        compiler_params=pltpu.CompilerParams(vmem_limit_bytes=48 * 2**20),
    )(table, qq, kv)


def return_kernel(out, d_out, attended, d_attended, ss, dss, rs, drs):
    block, x, y_hi, y_lo, y, z, core = coordinates()
    chip = my_chip(x, y)
    barrier = pltpu.get_barrier_semaphore()
    own = jnp.int32(0)
    for z_from in range(4):
        for g in range(2):
            for j in range(3):
                owner = (16 * j + block) // 6
                x_from, y_from = pick(owner, CHIP_X), 2 * g + owner // 4
                me = jnp.logical_and(jnp.logical_and(x_from == x, y_from == y), z == z_from)
                own = own + me.astype(jnp.int32)

                @pl.when(jnp.logical_not(me))
                def _():
                    pl.semaphore_signal(
                        barrier, inc=1, device_id=device(x_from, y_from, z_from, core), device_id_type=MESH
                    )

    pl.semaphore_wait(barrier, 24 - own)

    sent = []
    for i in range(3):
        job = 6 * chip + 2 * i + core
        j, b = job // 16, job % 16
        lanes = pl.ds(pl.multiple_of((6 * z + 3 * (y // 2) + j) * 128, 128), 128)
        for d in range(8):
            p = (d + 4 * y_lo + z) % 8
            rows = pl.ds(pl.multiple_of(p * CHUNK, CHUNK), CHUNK)
            me = jnp.logical_and(b == block, p == 4 * y_lo + z)
            for source, target, sends, recv in ((out, attended, ss, rs), (d_out, d_attended, dss, drs)):
                from_ref, to_ref = source.at[i, rows], target.at[:, lanes]
                remote = pltpu.make_async_remote_copy(
                    src_ref=from_ref, dst_ref=to_ref, send_sem=sends.at[i, d], recv_sem=recv,
                    device_id=(b, p), device_id_type=MESH,
                )

                @pl.when(me)
                def _():
                    pltpu.make_async_copy(from_ref, to_ref, recv).start()

                @pl.when(jnp.logical_not(me))
                def _():
                    remote.start()

                sent.append((me, remote))
    pltpu.make_async_copy(attended, attended, rs).wait()
    pltpu.make_async_copy(d_attended, d_attended, drs).wait()
    for me, remote in sent:

        @pl.when(jnp.logical_not(me))
        def _():
            remote.wait_send()


def bring_back(out, d_out):
    anywhere = pl.BlockSpec(memory_space=pl.ANY)
    dma = pltpu.SemaphoreType.DMA
    return pl.pallas_call(
        return_kernel,
        name="bring_back",
        out_shape=(jax.ShapeDtypeStruct((CHUNK, 3072), jnp.bfloat16),) * 2,
        in_specs=[anywhere] * 2,
        out_specs=(anywhere,) * 2,
        scratch_shapes=[dma((3, 8)), dma((3, 8)), dma, dma],
        compiler_params=pltpu.CompilerParams(collective_id=1, has_side_effects=True),
    )(out, d_out)


def on_device(queries, keys, values, d_queries, d_keys, d_values, positions, key_lists):
    pkv, pq, table = rotate_all(queries, keys, values, d_queries, d_keys, d_values, positions, key_lists)
    kv, qq = bring(pkv, pq)
    out, d_out = attend(table, qq, kv)
    return bring_back(out, d_out)


def solution(mesh):
    tokens = P(("blk", "head"), None)
    return jax.shard_map(
        on_device,
        mesh=mesh,
        in_specs=(tokens,) * 6 + (P(None, ("blk", "head")), P()),
        out_specs=(tokens, tokens),
        check_vma=False,
    )
```

profile of v0, /device:TPU:0, one launch (start us, length us, event | category | flops | bytes accessed | tf_op | source)
XLA Modules:
  0.0 324.3 jit_solution(3763189202046127812)
XLA Ops:
  0.6 0.8 copy.12.lists_ref
  1.4 1.1 copy-done.5
  2.5 1.1 copy-done.6
  3.7 1.1 copy-done.7
  4.8 1.1 copy-done.8
  5.9 1.1 copy-done.9
  7.1 1.1 copy-done.10
  8.2 0.8 copy-done.11
  9.0 0.7 copy-done.12
  9.6 0.7 copy-done.13
  10.3 4.0 %rotate.1 = (bf16[24,128,512]{2,1,0:T(8,128)(2,1)S(1)}, bf16[24,128,256]{2,1,0:T(8,128)(2,1)S(1)}, s32[6,5]{1,0:T(8,128)S(1)}) custom-call(s32[16,5]{1,0:T(8,128)S(1)} %copy.12.lists_ref, s32[3,128]{1,0:T(4,128)S(1)} %copy-done.12, f32[3,128]{1,0:T(4,128)S(1)} %copy-done.13, bf16[128,128]{1,0:T(8,128)(2,1)S(1)} %copy-done.11, ...), custom_call_target="tpu_custom_call" | custom-call | tf_op jit(solution)/shard_map/rotate/pallas_call | solution.py:144
  14.3 0.0 copy-start
  14.3 1.6 copy-done
  16.0 1.2 copy-done.1
  17.2 233.9 %bring.1 = (bf16[6,512,512]{2,1,0:T(8,128)(2,1)}, bf16[6,512,256]{2,1,0:T(8,128)(2,1)}, bf16[2,2,1024,512]{3,2,1,0:T(8,128)(2,1)}, bf16[2,2,1024,256]{3,2,1,0:T(...) custom-call(bf16[24,128,512]{2,1,0:T(8,128)(2,1)} %copy-done, bf16[24,128,256]{2,1,0:T(8,128)(2,1)} %copy-done.1), custom_call_target="tpu_custom_call" | custom-call | tf_op jit(solution)/shard_map/bring/pallas_call | solution.py:321
  251.1 0.0 copy-start.2
  251.1 1.4 copy-done.2
  252.5 35.0 %attend.1 = (bf16[3,1024,128]{2,1,0:T(8,128)(2,1)S(1)}, bf16[3,1024,128]{2,1,0:T(8,128)(2,1)S(1)}) custom-call(s32[6,5]{1,0:T(8,128)S(1)} %get-tuple-element.9.table_ref, bf16[3,1024,256]{2,1,0:T(8,128)(2,1)S(1)} %copy-done.2, bf16[12,1024,512]{2,1,0:T(8,128)(2,1)} %get-tuple-element.13.kv_ref), custom_call_target="tpu_custom_call" | custom-call | tf_op jit(solution)/shard_map/attend/pallas_call | solution.py:386
  287.5 0.0 copy-start.3
  287.5 0.9 copy-done.3
  288.4 0.9 copy-done.4
  289.3 30.9 %bring_back.1 = (bf16[128,3072]{1,0:T(8,128)(2,1)}, bf16[128,3072]{1,0:T(8,128)(2,1)}) custom-call(bf16[3,1024,128]{2,1,0:T(8,128)(2,1)} %copy-done.3, bf16[3,1024,128]{2,1,0:T(8,128)(2,1)} %copy-done.4), custom_call_target="tpu_custom_call" | custom-call | tf_op jit(solution)/shard_map/bring_back/pallas_call | solution.py:467
  320.2 2.1 copy.15
  322.3 2.1 copy.16
  (11 shorter events, 0.0 us)
Async XLA Ops:
  1.4 1.1 copy-start.5
  2.5 1.1 copy-start.6
  3.7 1.1 copy-start.7
  4.8 1.1 copy-start.8
  5.9 1.1 copy-start.9
  7.1 1.1 copy-start.10
  8.2 0.8 copy-start.11
  9.0 0.7 copy-start.12
  9.6 0.7 copy-start.13
  14.3 1.7 copy-start
  16.0 1.2 copy-start.1
  251.1 1.4 copy-start.2
  287.5 0.9 copy-start.3
  288.4 0.9 copy-start.4
where the time goes:
time: 326 us; the launch traced here: 324 us
  Pallas kernels  304 us (93%)
  local copies, waits for them, and re-layouts  19.8 us (6%)
    pallas_call x1, Pallas kernels, bring(): pl.pallas_call(bring_kernel, name='bring', out_shape=tuple((jax.ShapeDtyp...  234 us
    pallas_call x1, Pallas kernels, attend(): pl.pallas_call(attend_kernel, name='attend', grid_spec=pltpu.PrefetchScal...  35 us
    pallas_call x1, Pallas kernels, bring_back(): pl.pallas_call(return_kernel, name='bring_back', out_shape=(jax.ShapeDtyp...  30.9 us
    unnamed x31, local copies, waits for them, and re-layouts  19.8 us

commit v1 on v0

--- a/solution.py
+++ b/solution.py
@@ -17,7 +17,6 @@
 LOG2E = 1.4426950408889634
 CHIP_X = (0, 2, 3, 1, 2, 0, 1, 3)
 SLOTS = 12
-ORDER = (0, 5, 2, 3, 1, 4)
 
 
 def chip_runs():
@@ -164,13 +163,47 @@
     )
 
 
+KV_WAIT, KV_ROWS = (SLOTS + 4) * QB, (SLOTS + 7) * QB
+Q_PASS, Q_WAIT, Q_ROWS = 3 * QB, 7 * QB, 10 * QB
+CODES = [run_code(CHIP_AT[side][x], j) for j in range(3) for side in range(2) for x in range(4)]
+
+
+def window(x, side, j):
+    code = pick(8 * j + 4 * side + x, CODES)
+    return code // 4096, (code // 64) % 64, code % 64
+
+
+def wants(side, block):
+    return jnp.where(side == 0, block <= 10, block >= 5)
+
+
+def kv_place(x, side, j, block):
+    low, high, base = window(x, side, j)
+    inside = jnp.logical_and(block >= low, block <= high)
+    full = 1 if isinstance(j, int) and j == 1 else jnp.where(j == 1, 1, 0)
+    return jnp.where(inside, block - low + base, SLOTS + 2 * full + (block // 2) % 2)
+
+
+def q_place(x, j, block):
+    job = 16 * j + block
+    full = 1 if isinstance(j, int) and j == 1 else jnp.where(j == 1, 1, 0)
+    passing = Q_PASS + (2 * full + (block // 2) % 2) * QB
+    return jnp.where(pick(job // 6, CHIP_X) == x, (job % 6) // 2 * QB, passing)
+
+
+def at_rows(ref, first, count, step):
+    return ref.at[pl.ds(pl.multiple_of(first, step), count)]
+
+
 def bring_kernel(
-    pkv, pq, zkv, zq, ykv, yq, kv, qq,
+    pkv, pq, kv, qq,
     zs, zqs, ys, yqs, xs, xqs, fs, zr, zqr, yr, yqr, kr, qr, fr,
 ):
     block, x, y_hi, y_lo, y, z, core = coordinates()
     side = y % 2
     chip = my_chip(x, y)
+    always = block >= 0
+    no, both = jnp.logical_not, jnp.logical_and
 
     barrier = pltpu.get_barrier_semaphore()
     partners = (
@@ -185,148 +218,212 @@
 
     sent = []
 
-    def send(where, here, source, target, send_sem, recv_sem, to):
-        if here is not False:
-
-            @pl.when(jnp.logical_and(where, here))
-            def _():
-                pltpu.make_async_copy(source, target, recv_sem).start()
-
-        if here is not True:
-            away = where if here is False else jnp.logical_and(where, jnp.logical_not(here))
-            remote = pltpu.make_async_remote_copy(
-                src_ref=source, dst_ref=target, send_sem=send_sem, recv_sem=recv_sem, device_id=to, device_id_type=MESH
-            )
-
-            @pl.when(away)
-            def _():
-                remote.start()
-
-            sent.append((away, remote))
+    def send(where, source, target, send_sem, recv_sem, to):
+        remote = pltpu.make_async_remote_copy(
+            src_ref=source, dst_ref=target, send_sem=send_sem, recv_sem=recv_sem, device_id=to, device_id_type=MESH
+        )
+
+        @pl.when(where)
+        def _():
+            remote.start()
+
+        sent.append((where, remote))
 
     def arrived(where, target, recv_sem):
         @pl.when(where)
         def _():
             pltpu.make_async_copy(target, target, recv_sem).wait()
 
-    always = block >= 0
-    rows_z = pl.ds(pl.multiple_of(z * CHUNK, CHUNK), CHUNK)
-    for hh in ORDER:
+
+    def kv_after_z(hh, start, size):
+        g, j = hh // 3, hh % 3
+        stays = both(y_hi == g, side == j // 2 if j != 1 else wants(side, block))
+        in_place = kv_place(x, side, j, block) * QB + start + y_lo * (size // 2)
+        return jnp.where(stays, in_place, KV_WAIT + hh * 512 + start // 2)
+
+    def q_after_z(hh):
+        g, j = hh // 3, hh % 3
+        stays = both(y_hi == g, side == (16 * j + block) // 24)
+        return stays, jnp.where(stays, q_place(x, j, block) + y_lo * 512, Q_WAIT + hh * 512)
+
+    def z_kv(mid, part, start, size):
+        for hh in (1, 4) if mid else (0, 5, 2, 3):
+            count = size // 8
+            to_rows = at_rows(kv, kv_after_z(hh, start, size) + z * count, count, STEP // 8)
+            for d in (2, 1, 3, 0):
+                to = (z + d) % 4
+                from_rows = pkv.at[6 * to + hh, pl.ds(start // 8, count)]
+                if d:
+                    send(always, from_rows, to_rows, zs.at[hh, part, d], zr.at[hh, part], device(x, y, to, core))
+                else:
+                    pltpu.make_async_copy(from_rows, to_rows, zr.at[hh, part]).start()
+
+    def z_q(hh):
+        _, row = q_after_z(hh)
+        to_rows = at_rows(qq, row + z * CHUNK, CHUNK, CHUNK)
         for d in (2, 1, 3, 0):
             to = (z + d) % 4
-            head = 6 * to + hh
-            place = device(x, y, to, core)
-            send(always, d == 0, pkv.at[head], zkv.at[hh, rows_z], zs.at[hh, d], zr.at[hh], place)
-            send(always, d == 0, pq.at[head], zq.at[hh, rows_z], zqs.at[hh, d], zqr.at[hh], place)
-
-    rows_y = pl.ds(pl.multiple_of(y_lo * 512, 512), 512)
-
-    def step_y(hh):
+            if d:
+                send(always, pq.at[6 * to + hh], to_rows, zqs.at[hh, d], zqr.at[hh], device(x, y, to, core))
+            else:
+                pltpu.make_async_copy(pq.at[6 * to + hh], to_rows, zqr.at[hh]).start()
+
+    def y_kv(mid, part, start, size):
+        count = size // 2
+        for hh in (1, 4) if mid else (0, 5, 2, 3):
+            g, j = hh // 3, hh % 3
+            source = at_rows(kv, kv_after_z(hh, start, size), count, STEP // 2)
+            arrived(always, source, zr.at[hh, part])
+            for s in (0, 1) if mid else (j // 2,):
+                where = wants(jnp.int32(s), block) if mid else always
+                to = 2 * g + s
+                row = kv_place(x, s, j, block) * QB + start + y_lo * count
+                send(
+                    both(where, y != to), source, at_rows(kv, row, count, STEP // 2),
+                    ys.at[hh, s, part], yr.at[mid, y_hi, y_lo, part], device(x, to, z, core),
+                )
+
+    def y_q(hh):
         g, j = hh // 3, hh % 3
-        full = 1 if j == 1 else 0
-        arrived(always, zkv.at[hh], zr.at[hh])
-        for s in (0, 1):
-            if (j, s) in ((0, 1), (2, 0)):
-                continue
-            where = always if j != 1 else (block <= 10 if s == 0 else block >= 5)
-            to = 2 * g + s
-            send(
-                where, y == to, zkv.at[hh], ykv.at[full, y_hi, rows_y], ys.at[hh, s], yr.at[full, y_hi, y_lo],
-                device(x, to, z, core),
-            )
-        arrived(always, zq.at[hh], zqr.at[hh])
-        to = 2 * g + (16 * j + block) // 24
+        stays, row = q_after_z(hh)
+        source = at_rows(qq, row, 512, 512)
+        arrived(always, source, zqr.at[hh])
         send(
-            always, y == to, zq.at[hh], yq.at[full, y_hi, rows_y], yqs.at[hh], yqr.at[full, y_hi],
-            device(x, to, z, core),
+            no(stays), source, at_rows(qq, q_place(x, j, block) + y_lo * 512, 512, 512),
+            yqs.at[hh], yqr.at[j % 2, y_hi, y_lo], device(x, 2 * g + (16 * j + block) // 24, z, core),
         )
 
-    def step_x(full):
-        j = 1 if full else 2 * side
+    def x_kv(mid, part, start, size):
+        j = 1 if mid else 2 * side
         for t in (0, 1):
             here = 4 * x + 2 * t + core
-            came = always if full == 0 else jnp.logical_or(
-                jnp.logical_and(side == 0, here <= 10), jnp.logical_and(side == 1, here >= 5)
+            came = wants(side, here) if mid else always
+            place = kv_place(x, side, j, here)
+            row = place * QB + start
+            for half in (0, 1):
+                own = both(t == y_hi, half == y_lo)
+                rows = at_rows(kv, row + half * (size // 2), size // 2, STEP // 2)
+                arrived(both(came, no(own)), rows, yr.at[mid, t, half, part])
+            source = at_rows(kv, row, size, STEP)
+            for d in (2, 1, 3):
+                to = (x + d) % 4
+                low, high, base = window(to, side, j)
+                wanted = both(here >= low, here <= high)
+                slot = jnp.where(wanted, here - low + base, 0)
+                send(
+                    wanted, source, at_rows(kv, slot * QB + start, size, STEP),
+                    xs.at[mid, t, d, part], kr.at[slot, part], device(to, y, z, core),
+                )
+            kept = both(came, place < SLOTS)
+            slot = jnp.where(kept, place, 0)
+            rows = at_rows(kv, slot * QB + start, size, STEP)
+            send(kept, rows, rows, fs.at[mid, t, 0, part], fr.at[slot, part], device(x, y, z, 1 - core))
+
+    def x_q(full_or_mid):
+        mid = full_or_mid
+        j = 1 if mid else 2 * side
+        for t in (0, 1):
+            job = 16 * j + 4 * x + 2 * t + core
+            owned = job // 24 == side
+            row = q_place(x, j, 4 * x + 2 * t + core)
+            for half in (0, 1):
+                own = both(t == y_hi, half == y_lo)
+                arrived(both(owned, no(own)), at_rows(qq, row + half * 512, 512, 512), yqr.at[mid, t, half])
+            to = pick(job // 6, CHIP_X)
+            slot = (job % 6) // 2
+            send(
+                both(owned, to != x), at_rows(qq, row, QB, QB), at_rows(qq, slot * QB, QB, QB),
+                xqs.at[mid, t], qr.at[slot], device(to, y, z, core),
             )
-            for half in (0, 1):
-                rows = pl.ds(512 * half, 512)
-                arrived(came, ykv.at[full, t, rows], yr.at[full, t, half])
-                for d in (2, 1, 3, 0):
-                    to = (x + d) % 4
-                    code = pick(
-                        4 * side + to,
-                        [run_code(CHIP_AT[s][xx], 1 if full else 2 * s) for s in range(2) for xx in range(4)],
-                    )
-                    low, high, base = code // 4096, (code // 64) % 64, code % 64
-                    wanted = jnp.logical_and(here >= low, here <= high)
-                    slot = jnp.where(wanted, here - low + base, 0)
-                    send(
-                        wanted, d == 0, ykv.at[full, t, rows], kv.at[slot, rows], xs.at[full, t, half, d], kr.at[slot],
-                        device(to, y, z, core),
-                    )
-            job = 16 * j + here
-            owned = job // 24 == side
-            arrived(owned, yq.at[full, t], yqr.at[full, t])
-            owner = job // 6
-            to = pick(owner, CHIP_X)
-            place = (job % 6) // 2
-            send(
-                owned, x == to, yq.at[full, t], qq.at[place], xqs.at[full, t], qr.at[place],
-                device(to, y, z, core),
-            )
-
-    for hh in ORDER[:4]:
-        step_y(hh)
-    step_x(0)
-    for hh in ORDER[4:]:
-        step_y(hh)
-    step_x(1)
-
-    first = pick(chip, [RUNS[k][0][1] for k in range(8)])
-    count = pick(chip, [sum(r[2] - r[1] + 1 for r in RUNS[k]) for k in range(8)])
-    second = pick(chip, [RUNS[k][1][3] if len(RUNS[k]) > 1 else 63 for k in range(8)])
-    second_low = pick(chip, [RUNS[k][1][1] if len(RUNS[k]) > 1 else 0 for k in range(8)])
-
-    def slot_here(s):
-        held = jnp.where(s < second, first + s, second_low + s - second)
-        return s < count, held % 2 == core
-
-    for s in range(SLOTS):
-        used, mine = slot_here(s)
-        direct = jnp.logical_and(used, mine)
-        arrived(direct, kv.at[s], kr.at[s])
-        send(direct, False, kv.at[s], kv.at[s], fs.at[s], fr.at[s], device(x, y, z, 1 - core))
-    for s in range(SLOTS):
-        used, mine = slot_here(s)
-        arrived(jnp.logical_and(used, jnp.logical_not(mine)), kv.at[s], fr.at[s])
+
+    def wanted_here(mid, t, d, other):
+        low, high, base = window(x, side, 1 if mid else 2 * side)
+        from_block = 4 * ((x + d) % 4) + 2 * t + (1 - core if other else core)
+        wanted = both(from_block >= low, from_block <= high)
+        return wanted, jnp.where(wanted, from_block - low + base, 0)
+
+    def to_other_core(mid, part, start, size):
+        for d in (1, 3, 2):
+            for t in (0, 1):
+                wanted, slot = wanted_here(mid, t, d, False)
+                rows = at_rows(kv, slot * QB + start, size, STEP)
+                arrived(wanted, rows, kr.at[slot, part])
+                send(wanted, rows, rows, fs.at[mid, t, d, part], fr.at[slot, part], device(x, y, z, 1 - core))
+
+    stages = {"z": z_kv, "y": y_kv, "x": x_kv, "c": to_other_core}
+    stages_q = {"z": z_q, "y": y_q, "x": x_q}
+    for name, item in SCHEDULE:
+        if isinstance(item, tuple):
+            for mid in (0, 1):
+                stages[name](mid, *item)
+        else:
+            stages_q[name](item)
+
+    for part, start, size in PARTS:
+        for mid, t in ((0, 0), (0, 1), (1, 0), (1, 1)):
+            for d in (0, 1, 3, 2):
+                wanted, slot = wanted_here(mid, t, d, True)
+                arrived(wanted, at_rows(kv, slot * QB + start, size, STEP), fr.at[slot, part])
     for i in range(3):
-        arrived(always, qq.at[i], qr.at[i])
-    for away, remote in sent:
-
-        @pl.when(away)
+        b = (6 * chip + 2 * i + core) % 16
+        arrived(b // 4 != x, at_rows(qq, i * QB, QB, QB), qr.at[i])
+    for where, remote in sent:
+
+        @pl.when(where)
         def _():
             remote.wait_send()
+
+
+STEP = 128
+SIZES = (128, 128, 256, 256, 256)
+PARTS = [(part, sum(SIZES[:part]), size) for part, size in enumerate(SIZES)]
+Q_ORDER = (0, 5, 2, 3, 1, 4)
+
+
+def make_schedule(lead, lag_x, lag_c):
+    steps = [("kv", part) for part in PARTS] + [("q", Q_ORDER[2 * i : 2 * i + 2]) for i in range(3)]
+    schedule = []
+
+    def add(stage, index):
+        if 0 <= index < len(steps):
+            kind, item = steps[index]
+            if kind == "kv":
+                schedule.append((stage, item))
+            elif stage in "zy":
+                schedule.extend((stage, hh) for hh in item)
+
+    for step in range(lead):
+        add("z", step)
+    for step in range(len(steps) + max(lag_x, lag_c)):
+        add("y", step)
+        add("z", step + lead)
+        add("x", step - lag_x)
+        add("c", step - lag_c)
+    return schedule + [("x", 0), ("x", 1)]
+
+
+SCHEDULE = make_schedule(3, 1, 3)
 
 
 def bring(pkv, pq):
     anywhere = pl.BlockSpec(memory_space=pl.ANY)
     dma = pltpu.SemaphoreType.DMA
-    shapes = [
-        (6, 512, 512), (6, 512, 256), (2, 2, QB, 512), (2, 2, QB, 256), (SLOTS, QB, 512), (3, QB, 256),
-    ]
+    n = len(PARTS)
     sems = [
-        (6, 4), (6, 4), (6, 2), (6,), (2, 2, 2, 4), (2, 2), (SLOTS,),
-        (6,), (6,), (2, 2, 2), (2, 2), (SLOTS,), (3,), (SLOTS,),
+        (6, n, 4), (6, 4), (6, 2, n), (6,), (2, 2, 4, n), (2, 2), (2, 2, 4, n),
+        (6, n), (6,), (2, 2, 2, n), (2, 2, 2), (SLOTS, n), (3,), (SLOTS, n),
     ]
     return pl.pallas_call(
         bring_kernel,
         name="bring",
-        out_shape=tuple(jax.ShapeDtypeStruct(shape, jnp.bfloat16) for shape in shapes),
+        out_shape=(
+            jax.ShapeDtypeStruct((KV_ROWS, 512), jnp.bfloat16), jax.ShapeDtypeStruct((Q_ROWS, 256), jnp.bfloat16),
+        ),
         in_specs=[anywhere] * 2,
-        out_specs=(anywhere,) * len(shapes),
+        out_specs=(anywhere,) * 2,
         scratch_shapes=[dma(shape) for shape in sems],
         compiler_params=pltpu.CompilerParams(collective_id=0, has_side_effects=True),
-    )(pkv, pq)[4:]
+    )(pkv, pq)
 
 
 def attend_kernel(table_ref, q_ref, kv_ref, out_ref, d_out_ref, top_ref, total_ref, light_ref, tilt_ref, rows=256):
@@ -342,17 +439,17 @@
 
     @pl.when(table_ref[3 + i, s] == 1)
     def _():
-        both_keys = kv_ref[0, :, 0:256]
-        keys = kv_ref[0, :, 0:128]
-        both_values = kv_ref[0, :, 256:512]
+        both_keys = kv_ref[:, 0:256]
+        keys = kv_ref[:, 0:128]
+        both_values = kv_ref[:, 256:512]
         ones = jnp.ones((QB, 128), jnp.bfloat16)
-        values = jnp.concatenate([kv_ref[0, :, 256:384], ones], axis=1)
+        values = jnp.concatenate([kv_ref[:, 256:384], ones], axis=1)
         across = (((1,), (1,)), ((), ()))
 
         for part in range(QB // rows):
             at = pl.ds(part * rows, rows)
-            score = lax.dot_general(q_ref[0, at, 128:256], keys, across, preferred_element_type=jnp.float32)
-            d_score = lax.dot_general(q_ref[0, at, :], both_keys, across, preferred_element_type=jnp.float32)
+            score = lax.dot_general(q_ref[at, 128:256], keys, across, preferred_element_type=jnp.float32)
+            d_score = lax.dot_general(q_ref[at, :], both_keys, across, preferred_element_type=jnp.float32)
             old = top_ref[at, :]
             new = jnp.maximum(old, jnp.max(score, axis=1, keepdims=True))
             top_ref[at, :] = new
@@ -390,8 +487,8 @@
             num_scalar_prefetch=1,
             grid=(3, 5),
             in_specs=[
-                pl.BlockSpec((1, QB, 256), lambda i, s, table: (i, 0, 0)),
-                pl.BlockSpec((1, QB, 512), lambda i, s, table: (table[i, s], 0, 0)),
+                pl.BlockSpec((QB, 256), lambda i, s, table: (i, 0)),
+                pl.BlockSpec((QB, 512), lambda i, s, table: (table[i, s], 0)),
             ],
             out_specs=(out, out),
             scratch_shapes=[

time: 326 us -> 199 us (0.61)
  Pallas kernels: 304 us -> 177 us
    pallas_call x1, Pallas kernels: 234 us -> 97.8 us  [bring(): pl.pallas_call(bring_kernel, name='bring', out_shape=(jax.ShapeDtypeStruc...]
    pallas_call x1, Pallas kernels: 35 us -> 47.2 us  [attend(): pl.pallas_call(attend_kernel, name='attend', grid_spec=pltpu.PrefetchScal...]
    unnamed x31 -> x29, local copies, waits for them, and re-layouts: 19.8 us -> 18.5 us
where the time goes in v1:
time: 199 us; the launch traced here: 196 us
  Pallas kernels  177 us (89%)
  local copies, waits for them, and re-layouts  18.5 us (9%)
    pallas_call x1, Pallas kernels, bring(): pl.pallas_call(bring_kernel, name='bring', out_shape=(jax.ShapeDtypeStruc...  97.8 us
    pallas_call x1, Pallas kernels, attend(): pl.pallas_call(attend_kernel, name='attend', grid_spec=pltpu.PrefetchScal...  47.2 us
    pallas_call x1, Pallas kernels, bring_back(): pl.pallas_call(return_kernel, name='bring_back', out_shape=(jax.ShapeDtyp...  27.7 us
    unnamed x29, local copies, waits for them, and re-layouts  18.5 us
    pallas_call x1, Pallas kernels, rotate_all(): pl.pallas_call(rotate_kernel, name='rotate', grid=(steps,), out_shape=(ja...  3.99 us

profile of v1, /device:TPU:0, one launch (start us, length us, event | category | flops | bytes accessed | tf_op | source)
XLA Modules:
  0.0 195.9 jit_solution(8203741847122334438)
XLA Ops:
  0.6 0.8 copy.12.lists_ref
  1.4 0.0 copy-start.4
  1.4 1.1 copy-done.4
  2.5 0.0 copy-start.5
  2.5 1.1 copy-done.5
  3.7 1.1 copy-done.6
  4.8 1.1 copy-done.7
  5.9 1.1 copy-done.8
  7.1 1.1 copy-done.9
  8.2 0.8 copy-done.10
  9.0 0.7 copy-done.11
  9.6 0.7 copy-done.12
  10.3 4.0 %rotate.1 = (bf16[24,128,512]{2,1,0:T(8,128)(2,1)S(1)}, bf16[24,128,256]{2,1,0:T(8,128)(2,1)S(1)}, s32[6,5]{1,0:T(8,128)S(1)}) custom-call(s32[16,5]{1,0:T(8,128)S(1)} %copy.12.lists_ref, s32[3,128]{1,0:T(4,128)S(1)} %copy-done.11, f32[3,128]{1,0:T(4,128)S(1)} %copy-done.12, bf16[128,128]{1,0:T(8,128)(2,1)S(1)} %copy-done.10, ...), custom_call_target="tpu_custom_call" | custom-call | tf_op jit(solution)/shard_map/rotate/pallas_call | solution.py:143
  14.3 0.0 copy-start
  14.3 1.7 copy-done
  16.0 1.2 copy-done.1
  17.3 97.8 %bring.1 = (bf16[19456,512]{1,0:T(8,128)(2,1)}, bf16[10240,256]{1,0:T(8,128)(2,1)}) custom-call(bf16[24,128,512]{2,1,0:T(8,128)(2,1)} %copy-done, bf16[24,128,256]{2,1,0:T(8,128)(2,1)} %copy-done.1), custom_call_target="tpu_custom_call" | custom-call | tf_op jit(solution)/shard_map/bring/pallas_call | solution.py:416
  115.2 47.2 %attend.1 = (bf16[3,1024,128]{2,1,0:T(8,128)(2,1)S(1)}, bf16[3,1024,128]{2,1,0:T(8,128)(2,1)S(1)}) custom-call(s32[6,5]{1,0:T(8,128)S(1)} %get-tuple-element.9.table_ref, bf16[10240,256]{1,0:T(8,128)(2,1)} %get-tuple-element.12.q_ref, bf16[19456,512]{1,0:T(8,128)(2,1)} %get-tuple-element.13.kv_ref), custom_call_target="tpu_custom_call" | custom-call | tf_op jit(solution)/shard_map/attend/pallas_call | solution.py:483
  162.3 0.0 copy-start.2
  162.3 0.9 copy-done.2
  163.2 0.9 copy-done.3
  164.1 27.7 %bring_back.1 = (bf16[128,3072]{1,0:T(8,128)(2,1)}, bf16[128,3072]{1,0:T(8,128)(2,1)}) custom-call(bf16[3,1024,128]{2,1,0:T(8,128)(2,1)} %copy-done.2, bf16[3,1024,128]{2,1,0:T(8,128)(2,1)} %copy-done.3), custom_call_target="tpu_custom_call" | custom-call | tf_op jit(solution)/shard_map/bring_back/pallas_call | solution.py:564
  191.8 2.1 %copy.15 = bf16[128,3072]{1,0:T(8,128)(2,1)} copy(bf16[128,3072]{1,0:T(8,128)(2,1)} %get-tuple-element.18) | data formatting | bytes 1572864
  193.9 2.1 %copy.16 = bf16[128,3072]{1,0:T(8,128)(2,1)} copy(bf16[128,3072]{1,0:T(8,128)(2,1)} %get-tuple-element.19) | data formatting | bytes 1572864
  (9 shorter events, 0.0 us)
Async XLA Ops:
  1.4 1.1 copy-start.4
  2.5 1.1 copy-start.5
  3.7 1.1 copy-start.6
  4.8 1.1 copy-start.7
  5.9 1.1 copy-start.8
  7.1 1.1 copy-start.9
  8.2 0.8 copy-start.10
  9.0 0.7 copy-start.11
  9.6 0.7 copy-start.12
  14.3 1.7 copy-start
  16.0 1.2 copy-start.1
  162.3 0.9 copy-start.2
  163.2 0.9 copy-start.3

commit v2 on v1

v2 whole, which is shorter than its diff:
```python
import functools

import jax
import jax.numpy as jnp
import numpy as np
from jax import lax
from jax.experimental import pallas as pl
from jax.experimental.pallas import tpu as pltpu
from jax.sharding import PartitionSpec as P

MESH = pl.DeviceIdType.MESH
REACH = 3
BLOCKS = 16
CHUNK = 128
QB = 1024
SCALE = 128 ** (-0.5)
LOG2E = 1.4426950408889634
CHIP_X = (0, 2, 3, 1, 2, 0, 1, 3)
SLOTS = 12


def chip_runs():
    runs = []
    for k in range(8):
        mine, base = [], 0
        for j in range(3):
            blocks = [job % 16 for job in range(6 * k, 6 * k + 6) if job // 16 == j]
            if blocks:
                low, high = max(0, blocks[0] - REACH), min(BLOCKS - 1, blocks[-1] + REACH)
                mine.append((j, low, high, base))
                base += high - low + 1
        runs.append(mine)
    return runs


RUNS = chip_runs()
CHIP_AT = [[CHIP_X[4 * side : 4 * side + 4].index(x) + 4 * side for x in range(4)] for side in range(2)]


def pick(index, values):
    result = jnp.int32(values[0])
    for place, value in enumerate(values[1:], 1):
        if value != values[0]:
            result = jnp.where(index == place, jnp.int32(value), result)
    return result


def run_code(k, j):
    for head, low, high, base in RUNS[k]:
        if head == j:
            return (low * 64 + high) * 64 + base
    return (63 * 64) * 64


def coordinates():
    block = lax.axis_index("blk")
    part = lax.axis_index("head")
    x, y_hi, core = block // 4, (block // 2) % 2, block % 2
    y_lo, z = part // 4, part % 4
    return block, x, y_hi, y_lo, 2 * y_hi + y_lo, z, core


def device(x, y, z, core):
    return (4 * x + 2 * (y // 2) + core, 4 * (y % 2) + z)


def my_chip(x, y):
    return pick(4 * (y % 2) + x, CHIP_AT[0] + CHIP_AT[1])


def frequency_rows():
    tables = np.zeros((3, 128), np.float32)
    start = 0
    for axis_id, count, span in ((0, 22, 44), (1, 21, 42), (2, 21, 42)):
        for column in range(count):
            rate = 1.0 / 10000.0 ** (2.0 * column / span)
            tables[axis_id, 2 * (start + column)] = rate
            tables[axis_id, 2 * (start + column) + 1] = rate
        start += count
    return tables


def swap_table():
    table = np.zeros((128, 128), np.float32)
    for pair in range(64):
        table[2 * pair + 1, 2 * pair] = -1.0
        table[2 * pair, 2 * pair + 1] = 1.0
    return table


def rotate_kernel(
    lists_ref, spots_ref, rates_ref, swap_ref, q_ref, k_ref, v_ref, dq_ref, dk_ref, dv_ref,
    kv_ref, qq_ref, table_ref, cos_ref, sin_ref,
):
    heads = kv_ref.shape[0]

    @pl.when(pl.program_id(0) == 0)
    def _():
        spots = spots_ref[...].astype(jnp.float32)
        angle = jnp.zeros((CHUNK, 128), jnp.float32)
        for axis_id in range(3):
            column = jnp.broadcast_to(spots[axis_id : axis_id + 1, :], (128, CHUNK)).T
            angle = angle + column * rates_ref[axis_id : axis_id + 1, :]
        cos_ref[...] = jnp.cos(angle)
        sin_ref[...] = jnp.sin(angle)
        _, x, _, _, y, _, core = coordinates()
        chip = my_chip(x, y)
        for i in range(3):
            job = 6 * chip + 2 * i + core
            j, block = job // 16, job % 16
            code = pick(3 * chip + j, [run_code(k, h) for k in range(8) for h in range(3)])
            low, base = code // 4096, code % 64
            last = jnp.int32(0)
            for s in range(5):
                entry = lists_ref[block, s]
                listed = entry >= 0
                last = jnp.where(listed, entry - low + base, last)
                table_ref[i, s] = last
                table_ref[3 + i, s] = listed.astype(jnp.int32)

    cosine, sine, swap = cos_ref[...], sin_ref[...], swap_ref[...]

    def turned(ref, lanes):
        part = ref[:, lanes]
        swapped = jnp.dot(part, swap, preferred_element_type=jnp.float32)
        return (part.astype(jnp.float32) * cosine + swapped * sine).astype(jnp.bfloat16)

    for head in range(heads):
        lanes = slice(128 * head, 128 * head + 128)
        kv_ref[head, :, 0:128] = turned(k_ref, lanes)
        kv_ref[head, :, 128:256] = turned(dk_ref, lanes)
        kv_ref[head, :, 256:384] = v_ref[:, lanes]
        kv_ref[head, :, 384:512] = dv_ref[:, lanes]
        qq_ref[head, :, 0:128] = turned(dq_ref, lanes)
        qq_ref[head, :, 128:256] = turned(q_ref, lanes)


def rotate_all(queries, keys, values, d_queries, d_keys, d_values, positions, key_lists):
    group = 4
    steps = 24 // group
    whole = pl.BlockSpec(memory_space=pltpu.VMEM)
    columns = pl.BlockSpec((CHUNK, 128 * group), lambda i: (0, i))
    return pl.pallas_call(
        rotate_kernel,
        name="rotate",
        grid=(steps,),
        out_shape=(
            jax.ShapeDtypeStruct((24, CHUNK, 512), jnp.bfloat16),
            jax.ShapeDtypeStruct((24, CHUNK, 256), jnp.bfloat16),
            jax.ShapeDtypeStruct((6, 5), jnp.int32),
        ),
        in_specs=[pl.BlockSpec(memory_space=pltpu.SMEM), whole, whole, whole] + [columns] * 6,
        out_specs=(
            pl.BlockSpec((group, CHUNK, 512), lambda i: (i, 0, 0)),
            pl.BlockSpec((group, CHUNK, 256), lambda i: (i, 0, 0)),
            pl.BlockSpec(memory_space=pltpu.SMEM),
        ),
        scratch_shapes=[pltpu.VMEM((CHUNK, 128), jnp.float32)] * 2,
        compiler_params=pltpu.CompilerParams(vmem_limit_bytes=32 * 2**20),
    )(
        key_lists, positions, jnp.asarray(frequency_rows()), jnp.asarray(swap_table(), jnp.bfloat16),
        queries, keys, values, d_queries, d_keys, d_values,
    )


GROUP = 256
KV_WAIT = (SLOTS + 4) * GROUP
Q_PASS, Q_WAIT, Q_ROWS = 3 * QB, 7 * QB, 10 * QB
CODES = [run_code(CHIP_AT[side][x], j) for j in range(3) for side in range(2) for x in range(4)]


def window(x, side, j):
    code = pick(8 * j + 4 * side + x, CODES)
    return code // 4096, (code // 64) % 64, code % 64


def wants(side, block):
    return jnp.where(side == 0, block <= 10, block >= 5)


def kv_place(x, side, j, block):
    low, high, base = window(x, side, j)
    inside = jnp.logical_and(block >= low, block <= high)
    full = 1 if isinstance(j, int) and j == 1 else jnp.where(j == 1, 1, 0)
    return jnp.where(inside, block - low + base, SLOTS + 2 * full + (block // 2) % 2)


def q_place(x, j, block):
    job = 16 * j + block
    full = 1 if isinstance(j, int) and j == 1 else jnp.where(j == 1, 1, 0)
    passing = Q_PASS + (2 * full + (block // 2) % 2) * QB
    return jnp.where(pick(job // 6, CHIP_X) == x, (job % 6) // 2 * QB, passing)


def at_rows(ref, first, count, step):
    return ref.at[pl.ds(pl.multiple_of(first, step), count)]


def at_kv(ref, row, count, step):
    return ref.at[row // GROUP, pl.ds(pl.multiple_of(row % GROUP, step), count)]


def whole_kernel(
    table, pkv, pq, attended, d_attended,
    kv0, kv1, kv2, kv3, qq, out, d_out, top, total, light, tilt,
    zs, zqs, ys, yqs, xs, xqs, fs, zr, zqr, yr, yqr, kr, qr, fr, os, dos, orr, dor,
):
    quarters = (kv0, kv1, kv2, kv3)
    block, x, y_hi, y_lo, y, z, core = coordinates()
    side = y % 2
    chip = my_chip(x, y)
    always = block >= 0
    no, both = jnp.logical_not, jnp.logical_and

    barrier = pltpu.get_barrier_semaphore()
    partners = (
        [device(x, y, (z + d) % 4, core) for d in (1, 2, 3)]
        + [device(x, (y + d) % 4, z, core) for d in (1, 2, 3)]
        + [device((x + d) % 4, y, z, core) for d in (1, 2, 3)]
        + [device(x, y, z, 1 - core)]
    )
    for partner in partners:
        pl.semaphore_signal(barrier, inc=1, device_id=partner, device_id_type=MESH)
    own = jnp.int32(0)
    for z_from in range(4):
        for g in range(2):
            for j in range(3):
                owner = (16 * j + block) // 6
                x_from, y_from = pick(owner, CHIP_X), 2 * g + owner // 4
                me = both(both(x_from == x, y_from == y), z == z_from)
                own = own + me.astype(jnp.int32)

                @pl.when(no(me))
                def _():
                    pl.semaphore_signal(
                        barrier, inc=1, device_id=device(x_from, y_from, z_from, core), device_id_type=MESH
                    )

    pl.semaphore_wait(barrier, len(partners) + 24 - own)

    draining = []

    def send(where, source, target, send_sem, recv_sem, to):
        remote = pltpu.make_async_remote_copy(
            src_ref=source, dst_ref=target, send_sem=send_sem, recv_sem=recv_sem, device_id=to, device_id_type=MESH
        )

        @pl.when(where)
        def _():
            if draining:
                remote.wait_send()
            else:
                remote.start()

    def keep(source, target, sem):
        if not draining:
            pltpu.make_async_copy(source, target, sem).start()

    def arrived(where, target, recv_sem):
        if draining:
            return

        @pl.when(where)
        def _():
            pltpu.make_async_copy(target, target, recv_sem).wait()


    def kv_after_z(hh, first, size):
        g, j = hh // 3, hh % 3
        stays = both(y_hi == g, side == j // 2 if j != 1 else wants(side, block))
        in_place = kv_place(x, side, j, block) * GROUP + first + y_lo * (size // 2)
        return jnp.where(stays, in_place, KV_WAIT + hh * (GROUP // 2) + first // 2)

    def q_after_z(hh):
        g, j = hh // 3, hh % 3
        stays = both(y_hi == g, side == (16 * j + block) // 24)
        return stays, jnp.where(stays, q_place(x, j, block) + y_lo * 512, Q_WAIT + hh * 512)

    def z_kv(mid, part, start, size):
        kv, first = quarters[start // GROUP], start % GROUP
        for hh in (1, 4) if mid else (0, 5, 2, 3):
            count = size // 8
            to_rows = at_kv(kv, kv_after_z(hh, first, size) + z * count, count, STEP // 8)
            for d in (2, 1, 3, 0):
                to = (z + d) % 4
                from_rows = pkv.at[6 * to + hh, pl.ds(start // 8, count)]
                if d:
                    send(always, from_rows, to_rows, zs.at[hh, part, d], zr.at[hh, part], device(x, y, to, core))
                else:
                    keep(from_rows, to_rows, zr.at[hh, part])

    def z_q(hh):
        _, row = q_after_z(hh)
        to_rows = at_rows(qq, row + z * CHUNK, CHUNK, CHUNK)
        for d in (2, 1, 3, 0):
            to = (z + d) % 4
            if d:
                send(always, pq.at[6 * to + hh], to_rows, zqs.at[hh, d], zqr.at[hh], device(x, y, to, core))
            else:
                keep(pq.at[6 * to + hh], to_rows, zqr.at[hh])

    def y_kv(mid, part, start, size):
        kv, first = quarters[start // GROUP], start % GROUP
        count = size // 2
        for hh in (1, 4) if mid else (0, 5, 2, 3):
            g, j = hh // 3, hh % 3
            source = at_kv(kv, kv_after_z(hh, first, size), count, STEP // 2)
            arrived(always, source, zr.at[hh, part])
            for s in (0, 1) if mid else (j // 2,):
                where = wants(jnp.int32(s), block) if mid else always
                to = 2 * g + s
                row = kv_place(x, s, j, block) * GROUP + first + y_lo * count
                send(
                    both(where, y != to), source, at_kv(kv, row, count, STEP // 2),
                    ys.at[hh, s, part], yr.at[mid, y_hi, y_lo, part], device(x, to, z, core),
                )

    def y_q(hh):
        g, j = hh // 3, hh % 3
        stays, row = q_after_z(hh)
        source = at_rows(qq, row, 512, 512)
        arrived(always, source, zqr.at[hh])
        send(
            no(stays), source, at_rows(qq, q_place(x, j, block) + y_lo * 512, 512, 512),
            yqs.at[hh], yqr.at[j % 2, y_hi, y_lo], device(x, 2 * g + (16 * j + block) // 24, z, core),
        )

    def x_kv(mid, part, start, size):
        kv, first = quarters[start // GROUP], start % GROUP
        j = 1 if mid else 2 * side
        for t in (0, 1):
            here = 4 * x + 2 * t + core
            came = wants(side, here) if mid else always
            place = kv_place(x, side, j, here)
            row = place * GROUP + first
            for half in (0, 1):
                own = both(t == y_hi, half == y_lo)
                rows = at_kv(kv, row + half * (size // 2), size // 2, STEP // 2)
                arrived(both(came, no(own)), rows, yr.at[mid, t, half, part])
            source = at_kv(kv, row, size, STEP)
            for d in (2, 1, 3):
                to = (x + d) % 4
                low, high, base = window(to, side, j)
                wanted = both(here >= low, here <= high)
                slot = jnp.where(wanted, here - low + base, 0)
                send(
                    wanted, source, at_kv(kv, slot * GROUP + first, size, STEP),
                    xs.at[mid, t, d, part], kr.at[slot, part], device(to, y, z, core),
                )
            kept = both(came, place < SLOTS)
            slot = jnp.where(kept, place, 0)
            rows = at_kv(kv, slot * GROUP + first, size, STEP)
            send(kept, rows, rows, fs.at[mid, t, 0, part], fr.at[slot, part], device(x, y, z, 1 - core))

    def x_q(full_or_mid):
        mid = full_or_mid
        j = 1 if mid else 2 * side
        for t in (0, 1):
            job = 16 * j + 4 * x + 2 * t + core
            owned = job // 24 == side
            row = q_place(x, j, 4 * x + 2 * t + core)
            for half in (0, 1):
                own = both(t == y_hi, half == y_lo)
                arrived(both(owned, no(own)), at_rows(qq, row + half * 512, 512, 512), yqr.at[mid, t, half])
            to = pick(job // 6, CHIP_X)
            slot = (job % 6) // 2
            send(
                both(owned, to != x), at_rows(qq, row, QB, QB), at_rows(qq, slot * QB, QB, QB),
                xqs.at[mid, t], qr.at[slot], device(to, y, z, core),
            )

    def wanted_here(mid, t, d, other):
        low, high, base = window(x, side, 1 if mid else 2 * side)
        from_block = 4 * ((x + d) % 4) + 2 * t + (1 - core if other else core)
        wanted = both(from_block >= low, from_block <= high)
        return wanted, jnp.where(wanted, from_block - low + base, 0)

    def to_other_core(mid, part, start, size):
        kv, first = quarters[start // GROUP], start % GROUP
        for d in (1, 3, 2):
            for t in (0, 1):
                wanted, slot = wanted_here(mid, t, d, False)
                rows = at_kv(kv, slot * GROUP + first, size, STEP)
                arrived(wanted, rows, kr.at[slot, part])
                send(wanted, rows, rows, fs.at[mid, t, d, part], fr.at[slot, part], device(x, y, z, 1 - core))

    stages = {"z": z_kv, "y": y_kv, "x": x_kv, "c": to_other_core}
    stages_q = {"z": z_q, "y": y_q, "x": x_q}

    def go(step):
        name, item = step
        if isinstance(item, tuple):
            for mid in (0, 1):
                stages[name](mid, *item)
        else:
            stages_q[name](item)

    def complete(part, start, size):
        kv, first = quarters[start // GROUP], start % GROUP
        for mid, t in ((0, 0), (0, 1), (1, 0), (1, 1)):
            for d in (0, 1, 3, 2):
                wanted, slot = wanted_here(mid, t, d, True)
                arrived(wanted, at_kv(kv, slot * GROUP + first, size, STEP), fr.at[slot, part])

    def attend(quarter, tile):
        i = tile // (QB // TILE)
        at = pl.ds(pl.multiple_of(tile * TILE, TILE), TILE)
        kv = quarters[quarter]
        held = [kv[table[i, s]] for s in range(5)]
        absent = [jnp.where(table[3 + i, s] == 1, 0.0, 1e32) for s in range(5)]
        both_keys = jnp.concatenate([block_rows[:, 0:256] for block_rows in held], axis=0)
        both_values = jnp.concatenate([block_rows[:, 256:512] for block_rows in held], axis=0)
        ones = jnp.ones((5 * GROUP, 128), jnp.bfloat16)
        values = jnp.concatenate([both_values[:, 0:128], ones], axis=1)
        across = (((1,), (1,)), ((), ()))
        rows = qq[at, :]
        score = lax.dot_general(
            rows[:, 128:256], both_keys[:, 0:128], across, preferred_element_type=jnp.float32
        )
        d_score = lax.dot_general(rows, both_keys, across, preferred_element_type=jnp.float32)
        parts = [score[:, s * GROUP : (s + 1) * GROUP] for s in range(5)]
        tops = [jnp.max(parts[s], axis=1, keepdims=True) - absent[s] for s in range(5)]
        peak = functools.reduce(jnp.maximum, tops)
        if quarter:
            old = top[at, :]
            new = jnp.maximum(old, peak)
            fade = jnp.exp2((old - new) * (SCALE * LOG2E))
            fade2 = jnp.concatenate([fade, fade], axis=1)
        else:
            new = jnp.broadcast_to(peak, (TILE, 128))
        weight = jnp.concatenate(
            [jnp.exp2((parts[s] - (new[:, 0:1] + absent[s])) * (SCALE * LOG2E)) for s in range(5)], axis=1
        )
        tilted = weight * d_score
        sums = weight[:, 0:128]
        for c in range(1, 5 * GROUP // 128):
            sums = sums + weight[:, 128 * c : 128 * c + 128]
        lit = jnp.dot(weight.astype(jnp.bfloat16), both_values, preferred_element_type=jnp.float32)
        leaned = jnp.dot(tilted.astype(jnp.bfloat16), values, preferred_element_type=jnp.float32)
        if quarter:
            sums = total[at, :] * fade + sums
            lit = light[at, :] * fade2 + lit
            leaned = tilt[at, :] * fade2 + leaned
        if quarter < 3:
            top[at, :] = new
            total[at, :] = sums
            light[at, :] = lit
            tilt[at, :] = leaned
        else:
            inverse = 1.0 / jnp.sum(sums, axis=1, keepdims=True)
            result = lit[:, 0:128] * inverse
            moved = lit[:, 128:256] + SCALE * leaned[:, 0:128]
            slope = SCALE * leaned[:, 128:256]
            out[at, :] = result.astype(jnp.bfloat16)
            d_out[at, :] = (moved * inverse - slope * inverse * result).astype(jnp.bfloat16)

    def give_back(i):
        job = 6 * chip + 2 * i + core
        j, b = job // 16, job % 16
        lanes = pl.ds(pl.multiple_of((6 * z + 3 * (y // 2) + j) * 128, 128), 128)
        for d in range(8):
            p = (d + 4 * y_lo + z) % 8
            me = both(b == block, p == 4 * y_lo + z)
            for source, target, sends, recv in ((out, attended, os, orr), (d_out, d_attended, dos, dor)):
                from_ref, to_ref = at_rows(source, i * QB + p * CHUNK, CHUNK, CHUNK), target.at[:, lanes]
                if not draining:

                    @pl.when(me)
                    def _():
                        pltpu.make_async_copy(from_ref, to_ref, recv).start()

                send(no(me), from_ref, to_ref, sends.at[i, d], recv, (b, p))

    for quarter in range(4):
        before, during = SCHEDULE[quarter]
        for step in before:
            go(step)
        if quarter == 0:
            for i in range(3):
                b = (6 * chip + 2 * i + core) % 16
                arrived(b // 4 != x, at_rows(qq, i * QB, QB, QB), qr.at[i])
        for part, start, size in PARTS:
            if start // GROUP == quarter:
                complete(part, start, size)

        @pl.loop(0, 3 * QB // TILE)
        def _(tile):
            attend(quarter, tile)
            for turn, step in during:

                @pl.when(tile == turn)
                def _():
                    go(step)

            if quarter == 3:

                @pl.when(tile % (QB // TILE) == QB // TILE - 1)
                def _():
                    give_back(tile // (QB // TILE))

    pltpu.make_async_copy(attended, attended, orr).wait()
    pltpu.make_async_copy(d_attended, d_attended, dor).wait()
    draining.append(True)
    for before, during in SCHEDULE:
        for step in before + [step for _, step in during]:
            go(step)

    @pl.loop(0, 3)
    def _(i):
        give_back(i)


STEP = 128
TILE = 512
SIZES = (128, 128, 256, 256, 256)
PARTS = [(part, sum(SIZES[:part]), size) for part, size in enumerate(SIZES)]


def make_schedule(lead=3, lag_x=1, lag_c=3):
    kv = [("kv", part) for part in PARTS]
    queries = [("q", pair) for pair in ((0, 5), (2, 3), (1, 4))]
    steps = [kv[0], queries[0], kv[1], queries[1], kv[2], queries[2], kv[3], kv[4]]

    def one(stage, index):
        if not 0 <= index < len(steps):
            return []
        kind, item = steps[index]
        if kind == "kv":
            return [(stage, item)]
        if stage in "zy":
            return [(stage, hh) for hh in item]
        if stage == "x" and index == 3:
            return [("x", 0)]
        if stage == "x" and index == 5:
            return [("x", 1)]
        return []

    def turn(step):
        return one("y", step) + one("z", step + lead) + one("x", step - lag_x) + one("c", step - lag_c)

    first = [step for i in range(lead) for step in one("z", i)]
    for i in range(7):
        first += turn(i)
    y7, x6, c4 = one("y", 7), one("x", 6), one("c", 4)
    x7, c6, c7 = one("x", 7), one("c", 6), one("c", 7)
    return [
        (first, [(0, step) for step in y7] + [(1, step) for step in x6] + [(3, step) for step in c4]),
        ([], [(0, step) for step in x7] + [(3, step) for step in c6]),
        ([], [(3, step) for step in c7]),
        ([], []),
    ]


SCHEDULE = make_schedule()


def bring_attend_return(table, pkv, pq):
    anywhere = pl.BlockSpec(memory_space=pl.ANY)
    dma, vmem = pltpu.SemaphoreType.DMA, pltpu.VMEM
    n = len(PARTS)
    sems = [
        (6, n, 4), (6, 4), (6, 2, n), (6,), (2, 2, 4, n), (2, 2), (2, 2, 4, n),
        (6, n), (6,), (2, 2, 2, n), (2, 2, 2), (SLOTS, n), (3,), (SLOTS, n), (3, 8), (3, 8),
    ]
    return pl.pallas_call(
        whole_kernel,
        name="bring_attend_return",
        out_shape=(jax.ShapeDtypeStruct((CHUNK, 3072), jnp.bfloat16),) * 2,
        in_specs=[pl.BlockSpec(memory_space=pltpu.SMEM), anywhere, anywhere],
        out_specs=(anywhere,) * 2,
        scratch_shapes=[vmem((SLOTS + 7, GROUP, 512), jnp.bfloat16)] * 4
        + [vmem((Q_ROWS, 256), jnp.bfloat16)]
        + [vmem((3 * QB, 128), jnp.bfloat16)] * 2
        + [vmem((3 * QB, 128), jnp.float32)] * 2
        + [vmem((3 * QB, 256), jnp.float32)] * 2
        + [dma(shape) for shape in sems]
        + [dma, dma],
        compiler_params=pltpu.CompilerParams(
            collective_id=0, has_side_effects=True, vmem_limit_bytes=62 * 2**20
        ),
    )(table, pkv, pq)


def on_device(queries, keys, values, d_queries, d_keys, d_values, positions, key_lists):
    pkv, pq, table = rotate_all(queries, keys, values, d_queries, d_keys, d_values, positions, key_lists)
    return bring_attend_return(table, pkv, pq)


def solution(mesh):
    tokens = P(("blk", "head"), None)
    return jax.shard_map(
        on_device,
        mesh=mesh,
        in_specs=(tokens,) * 6 + (P(None, ("blk", "head")), P()),
        out_specs=(tokens, tokens),
        check_vma=False,
    )
```

time: 199 us -> 185 us (0.930); the launches traced: 196 us -> 184 us
  Pallas kernels: 177 us -> 167 us
    pallas_call x3 -> x1, Pallas kernels: 173 us -> 163 us  [bring_attend_return(): pl.pallas_call(whole_kernel, name='bring_attend_return', out_shape=(jax.S...]
    unnamed x29 -> x27, local copies, waits for them, and re-layouts: 18.5 us -> 17.2 us
where the time goes in v2:
time: 185 us; the launch traced here: 184 us
  Pallas kernels  167 us (90%)
  local copies, waits for them, and re-layouts  17.2 us (9%)
    pallas_call x1, Pallas kernels, bring_attend_return(): pl.pallas_call(whole_kernel, name='bring_attend_return', out_shape=(jax.S...  163 us
    unnamed x27, local copies, waits for them, and re-layouts  17.2 us
    pallas_call x1, Pallas kernels, rotate_all(): pl.pallas_call(rotate_kernel, name='rotate', grid=(steps,), out_shape=(ja...  3.99 us

profile of v2, /device:TPU:0, one launch (start us, length us, event | category | flops | bytes accessed | tf_op | source)
XLA Modules:
  0.0 184.4 jit_solution(10429503095278689051)
XLA Ops:
  0.6 0.8 copy.12.lists_ref
  1.4 0.0 copy-start.2
  1.4 1.1 copy-done.2
  2.5 0.0 copy-start.3
  2.5 1.1 copy-done.3
  3.7 0.0 copy-start.4
  3.7 1.1 copy-done.4
  4.8 1.1 copy-done.5
  5.9 0.0 copy-start.6
  5.9 1.1 copy-done.6
  7.1 0.0 copy-start.7
  7.1 1.1 copy-done.7
  8.2 0.0 copy-start.8
  8.2 0.8 copy-done.8
  9.0 0.7 copy-done.10
  9.6 0.7 copy-done.11
  10.3 4.0 %rotate.1 = (bf16[24,128,512]{2,1,0:T(8,128)(2,1)S(1)}, bf16[24,128,256]{2,1,0:T(8,128)(2,1)S(1)}, s32[6,5]{1,0:T(8,128)S(1)}) custom-call(s32[16,5]{1,0:T(8,128)S(1)} %copy.12.lists_ref, s32[3,128]{1,0:T(4,128)S(1)} %copy-done.10, f32[3,128]{1,0:T(4,128)S(1)} %copy-done.11, bf16[128,128]{1,0:T(8,128)(2,1)S(1)} %copy-done.8, ...), custom_call_target="tpu_custom_call" | custom-call | tf_op jit(solution)/shard_map/rotate/pallas_call | solution.py:143
  14.3 0.0 copy-start
  14.3 1.6 copy-done
  16.0 1.2 copy-done.1
  17.1 0.6 copy-done.9
  17.7 162.6 %bring_attend_return.1 = (bf16[128,3072]{1,0:T(8,128)(2,1)}, bf16[128,3072]{1,0:T(8,128)(2,1)}) custom-call(s32[6,5]{1,0:T(8,128)} %copy-done.9, bf16[24,128,512]{2,1,0:T(8,128)(2,1)} %copy-done, bf16[24,128,256]{2,1,0:T(8,128)(2,1)} %copy-done.1), custom_call_target="tpu_custom_call" | custom-call | tf_op jit(solution)/shard_map/bring_attend_return/pallas_call | solution.py:565
  180.3 2.1 %copy.15 = bf16[128,3072]{1,0:T(8,128)(2,1)} copy(bf16[128,3072]{1,0:T(8,128)(2,1)} %get-tuple-element.10) | data formatting | bytes 1572864
  182.3 2.1 %copy.16 = bf16[128,3072]{1,0:T(8,128)(2,1)} copy(bf16[128,3072]{1,0:T(8,128)(2,1)} %get-tuple-element.11) | data formatting | bytes 1572864
  (5 shorter events, 0.0 us)
Async XLA Ops:
  1.4 1.1 copy-start.2
  2.5 1.1 copy-start.3
  3.7 1.1 copy-start.4
  4.8 1.1 copy-start.5
  5.9 1.1 copy-start.6
  7.1 1.1 copy-start.7
  8.2 0.8 copy-start.8
  9.0 0.7 copy-start.10
  9.6 0.7 copy-start.11
  14.3 1.6 copy-start
  16.0 1.2 copy-start.1
  17.1 0.6 copy-start.9

commit v3 on v2

--- a/solution.py
+++ b/solution.py
@@ -156,7 +156,7 @@
             pl.BlockSpec(memory_space=pltpu.SMEM),
         ),
         scratch_shapes=[pltpu.VMEM((CHUNK, 128), jnp.float32)] * 2,
-        compiler_params=pltpu.CompilerParams(vmem_limit_bytes=32 * 2**20),
+        compiler_params=pltpu.CompilerParams(vmem_limit_bytes=62 * 2**20),
     )(
         key_lists, positions, jnp.asarray(frequency_rows()), jnp.asarray(swap_table(), jnp.bfloat16),
         queries, keys, values, d_queries, d_keys, d_values,
@@ -201,9 +201,9 @@
 
 
 def whole_kernel(
-    table, pkv, pq, attended, d_attended,
-    kv0, kv1, kv2, kv3, qq, out, d_out, top, total, light, tilt,
-    zs, zqs, ys, yqs, xs, xqs, fs, zr, zqr, yr, yqr, kr, qr, fr, os, dos, orr, dor,
+    table, pkv, pq, results,
+    kv0, kv1, kv2, kv3, qq, out, top, total, light, tilt,
+    zs, zqs, ys, yqs, xs, xqs, fs, zr, zqr, yr, yqr, kr, qr, fr, os, done,
 ):
     quarters = (kv0, kv1, kv2, kv3)
     block, x, y_hi, y_lo, y, z, core = coordinates()
@@ -271,10 +271,14 @@
         in_place = kv_place(x, side, j, block) * GROUP + first + y_lo * (size // 2)
         return jnp.where(stays, in_place, KV_WAIT + hh * (GROUP // 2) + first // 2)
 
-    def q_after_z(hh):
-        g, j = hh // 3, hh % 3
+    def head_of(place, b):
+        return (2 * (place + 3 - (b // 2) % 3)) % 3
+
+    def q_after_z(place, g):
+        j = head_of(place, block)
         stays = both(y_hi == g, side == (16 * j + block) // 24)
-        return stays, jnp.where(stays, q_place(x, j, block) + y_lo * 512, Q_WAIT + hh * 512)
+        row = jnp.where(stays, q_place(x, j, block) + y_lo * 512, Q_WAIT + (3 * g + j) * 512)
+        return j, stays, row
 
     def z_kv(mid, part, start, size):
         kv, first = quarters[start // GROUP], start % GROUP
@@ -289,15 +293,19 @@
                 else:
                     keep(from_rows, to_rows, zr.at[hh, part])
 
-    def z_q(hh):
-        _, row = q_after_z(hh)
-        to_rows = at_rows(qq, row + z * CHUNK, CHUNK, CHUNK)
-        for d in (2, 1, 3, 0):
-            to = (z + d) % 4
-            if d:
-                send(always, pq.at[6 * to + hh], to_rows, zqs.at[hh, d], zqr.at[hh], device(x, y, to, core))
-            else:
-                keep(pq.at[6 * to + hh], to_rows, zqr.at[hh])
+    def z_q(place):
+        for g in range(2):
+            j, _, row = q_after_z(place, g)
+            to_rows = at_rows(qq, row + z * CHUNK, CHUNK, CHUNK)
+            for d in (2, 1, 3, 0):
+                to = (z + d) % 4
+                from_rows = pq.at[6 * to + 3 * g + j]
+                if d:
+                    send(
+                        always, from_rows, to_rows, zqs.at[place, g, d], zqr.at[place, g], device(x, y, to, core)
+                    )
+                else:
+                    keep(from_rows, to_rows, zqr.at[place, g])
 
     def y_kv(mid, part, start, size):
         kv, first = quarters[start // GROUP], start % GROUP
@@ -315,15 +323,15 @@
                     ys.at[hh, s, part], yr.at[mid, y_hi, y_lo, part], device(x, to, z, core),
                 )
 
-    def y_q(hh):
-        g, j = hh // 3, hh % 3
-        stays, row = q_after_z(hh)
-        source = at_rows(qq, row, 512, 512)
-        arrived(always, source, zqr.at[hh])
-        send(
-            no(stays), source, at_rows(qq, q_place(x, j, block) + y_lo * 512, 512, 512),
-            yqs.at[hh], yqr.at[j % 2, y_hi, y_lo], device(x, 2 * g + (16 * j + block) // 24, z, core),
-        )
+    def y_q(place):
+        for g in range(2):
+            j, stays, row = q_after_z(place, g)
+            source = at_rows(qq, row, 512, 512)
+            arrived(always, source, zqr.at[place, g])
+            send(
+                no(stays), source, at_rows(qq, q_place(x, j, block) + y_lo * 512, 512, 512),
+                yqs.at[place, g], yqr.at[place, y_hi, y_lo], device(x, 2 * g + (16 * j + block) // 24, z, core),
+            )
 
     def x_kv(mid, part, start, size):
         kv, first = quarters[start // GROUP], start % GROUP
@@ -352,21 +360,20 @@
             rows = at_kv(kv, slot * GROUP + first, size, STEP)
             send(kept, rows, rows, fs.at[mid, t, 0, part], fr.at[slot, part], device(x, y, z, 1 - core))
 
-    def x_q(full_or_mid):
-        mid = full_or_mid
-        j = 1 if mid else 2 * side
+    def x_q(place):
         for t in (0, 1):
-            job = 16 * j + 4 * x + 2 * t + core
+            here = 4 * x + 2 * t + core
+            j = head_of(place, here)
+            job = 16 * j + here
             owned = job // 24 == side
-            row = q_place(x, j, 4 * x + 2 * t + core)
+            row = q_place(x, j, here)
             for half in (0, 1):
                 own = both(t == y_hi, half == y_lo)
-                arrived(both(owned, no(own)), at_rows(qq, row + half * 512, 512, 512), yqr.at[mid, t, half])
+                arrived(both(owned, no(own)), at_rows(qq, row + half * 512, 512, 512), yqr.at[place, t, half])
             to = pick(job // 6, CHIP_X)
-            slot = (job % 6) // 2
             send(
-                both(owned, to != x), at_rows(qq, row, QB, QB), at_rows(qq, slot * QB, QB, QB),
-                xqs.at[mid, t], qr.at[slot], device(to, y, z, core),
+                both(owned, to != x), at_rows(qq, row, QB, QB), at_rows(qq, place * QB, QB, QB),
+                xqs.at[place, t], qr.at[place], device(to, y, z, core),
             )
 
     def wanted_here(mid, t, d, other):
@@ -402,9 +409,8 @@
                 wanted, slot = wanted_here(mid, t, d, True)
                 arrived(wanted, at_kv(kv, slot * GROUP + first, size, STEP), fr.at[slot, part])
 
-    def attend(quarter, tile):
-        i = tile // (QB // TILE)
-        at = pl.ds(pl.multiple_of(tile * TILE, TILE), TILE)
+    def attend(quarter, i):
+        at = pl.ds(pl.multiple_of(i * QB, QB), QB)
         kv = quarters[quarter]
         held = [kv[table[i, s]] for s in range(5)]
         absent = [jnp.where(table[3 + i, s] == 1, 0.0, 1e32) for s in range(5)]
@@ -427,7 +433,7 @@
             fade = jnp.exp2((old - new) * (SCALE * LOG2E))
             fade2 = jnp.concatenate([fade, fade], axis=1)
         else:
-            new = jnp.broadcast_to(peak, (TILE, 128))
+            new = jnp.broadcast_to(peak, (QB, 128))
         weight = jnp.concatenate(
             [jnp.exp2((parts[s] - (new[:, 0:1] + absent[s])) * (SCALE * LOG2E)) for s in range(5)], axis=1
         )
@@ -451,59 +457,50 @@
             result = lit[:, 0:128] * inverse
             moved = lit[:, 128:256] + SCALE * leaned[:, 0:128]
             slope = SCALE * leaned[:, 128:256]
-            out[at, :] = result.astype(jnp.bfloat16)
-            d_out[at, :] = (moved * inverse - slope * inverse * result).astype(jnp.bfloat16)
+            out[at, 0:128] = result.astype(jnp.bfloat16)
+            out[at, 128:256] = (moved * inverse - slope * inverse * result).astype(jnp.bfloat16)
 
     def give_back(i):
         job = 6 * chip + 2 * i + core
         j, b = job // 16, job % 16
-        lanes = pl.ds(pl.multiple_of((6 * z + 3 * (y // 2) + j) * 128, 128), 128)
+        head = 6 * z + 3 * (y // 2) + j
         for d in range(8):
             p = (d + 4 * y_lo + z) % 8
             me = both(b == block, p == 4 * y_lo + z)
-            for source, target, sends, recv in ((out, attended, os, orr), (d_out, d_attended, dos, dor)):
-                from_ref, to_ref = at_rows(source, i * QB + p * CHUNK, CHUNK, CHUNK), target.at[:, lanes]
-                if not draining:
-
-                    @pl.when(me)
-                    def _():
-                        pltpu.make_async_copy(from_ref, to_ref, recv).start()
-
-                send(no(me), from_ref, to_ref, sends.at[i, d], recv, (b, p))
-
-    for quarter in range(4):
-        before, during = SCHEDULE[quarter]
-        for step in before:
-            go(step)
-        if quarter == 0:
-            for i in range(3):
-                b = (6 * chip + 2 * i + core) % 16
-                arrived(b // 4 != x, at_rows(qq, i * QB, QB, QB), qr.at[i])
-        for part, start, size in PARTS:
-            if start // GROUP == quarter:
-                complete(part, start, size)
-
-        @pl.loop(0, 3 * QB // TILE)
-        def _(tile):
-            attend(quarter, tile)
-            for turn, step in during:
-
-                @pl.when(tile == turn)
+            from_ref, to_ref = at_rows(out, i * QB + p * CHUNK, CHUNK, CHUNK), results.at[head]
+            if not draining:
+
+                @pl.when(me)
                 def _():
+                    pltpu.make_async_copy(from_ref, to_ref, done).start()
+
+            send(no(me), from_ref, to_ref, os.at[i, d], done, (b, p))
+
+    first, between = PROGRAM
+    for step in first:
+        go(step)
+
+    @pl.loop(0, 3)
+    def _(i):
+        b = (6 * chip + 2 * i + core) % 16
+        arrived(b // 4 != x, at_rows(qq, i * QB, QB, QB), qr.at[i])
+        for quarter in range(4):
+
+            @pl.when(i == 0)
+            def _():
+                for step in between[quarter]:
                     go(step)
-
-            if quarter == 3:
-
-                @pl.when(tile % (QB // TILE) == QB // TILE - 1)
-                def _():
-                    give_back(tile // (QB // TILE))
-
-    pltpu.make_async_copy(attended, attended, orr).wait()
-    pltpu.make_async_copy(d_attended, d_attended, dor).wait()
+                for part, start, size in PARTS:
+                    if start // GROUP == quarter:
+                        complete(part, start, size)
+
+            attend(quarter, i)
+        give_back(i)
+
+    pltpu.make_async_copy(results, results, done).wait()
     draining.append(True)
-    for before, during in SCHEDULE:
-        for step in before + [step for _, step in during]:
-            go(step)
+    for step in first + between[0] + between[1] + between[2] + between[3]:
+        go(step)
 
     @pl.loop(0, 3)
     def _(i):
@@ -511,47 +508,32 @@
 
 
 STEP = 128
-TILE = 512
 SIZES = (128, 128, 256, 256, 256)
 PARTS = [(part, sum(SIZES[:part]), size) for part, size in enumerate(SIZES)]
 
 
-def make_schedule(lead=3, lag_x=1, lag_c=3):
-    kv = [("kv", part) for part in PARTS]
-    queries = [("q", pair) for pair in ((0, 5), (2, 3), (1, 4))]
-    steps = [kv[0], queries[0], kv[1], queries[1], kv[2], queries[2], kv[3], kv[4]]
+def make_program(order, lead, lag_x, lag_c, before, where):
+    steps = [PARTS[int(c)] if c.isdigit() else "abc".index(c) for c in order]
 
     def one(stage, index):
-        if not 0 <= index < len(steps):
+        if not 0 <= index < len(steps) or (stage == "c" and not isinstance(steps[index], tuple)):
             return []
-        kind, item = steps[index]
-        if kind == "kv":
-            return [(stage, item)]
-        if stage in "zy":
-            return [(stage, hh) for hh in item]
-        if stage == "x" and index == 3:
-            return [("x", 0)]
-        if stage == "x" and index == 5:
-            return [("x", 1)]
-        return []
-
-    def turn(step):
-        return one("y", step) + one("z", step + lead) + one("x", step - lag_x) + one("c", step - lag_c)
+        return [(stage, steps[index])]
 
     first = [step for i in range(lead) for step in one("z", i)]
-    for i in range(7):
-        first += turn(i)
-    y7, x6, c4 = one("y", 7), one("x", 6), one("c", 4)
-    x7, c6, c7 = one("x", 7), one("c", 6), one("c", 7)
-    return [
-        (first, [(0, step) for step in y7] + [(1, step) for step in x6] + [(3, step) for step in c4]),
-        ([], [(0, step) for step in x7] + [(3, step) for step in c6]),
-        ([], [(3, step) for step in c7]),
-        ([], []),
+    turns = [
+        one("y", turn) + one("z", turn + lead) + one("x", turn - lag_x) + one("c", turn - lag_c)
+        for turn in range(len(steps) + max(lag_x, lag_c))
     ]
-
-
-SCHEDULE = make_schedule()
+    for turn in turns[:before]:
+        first += turn
+    between = [[] for _ in range(4)]
+    for place, turn in zip(where, turns[before:]):
+        between[place] += turn
+    return first, between
+
+
+PROGRAM = make_program("01234abc", 3, 1, 3, 7, (1, 2, 3, 3))
 
 
 def bring_attend_return(table, pkv, pq):
@@ -559,22 +541,22 @@
     dma, vmem = pltpu.SemaphoreType.DMA, pltpu.VMEM
     n = len(PARTS)
     sems = [
-        (6, n, 4), (6, 4), (6, 2, n), (6,), (2, 2, 4, n), (2, 2), (2, 2, 4, n),
-        (6, n), (6,), (2, 2, 2, n), (2, 2, 2), (SLOTS, n), (3,), (SLOTS, n), (3, 8), (3, 8),
+        (6, n, 4), (3, 2, 4), (6, 2, n), (3, 2), (2, 2, 4, n), (3, 2), (2, 2, 4, n),
+        (6, n), (3, 2), (2, 2, 2, n), (3, 2, 2), (SLOTS, n), (3,), (SLOTS, n), (3, 8),
     ]
     return pl.pallas_call(
         whole_kernel,
         name="bring_attend_return",
-        out_shape=(jax.ShapeDtypeStruct((CHUNK, 3072), jnp.bfloat16),) * 2,
+        out_shape=jax.ShapeDtypeStruct((24, CHUNK, 256), jnp.bfloat16),
         in_specs=[pl.BlockSpec(memory_space=pltpu.SMEM), anywhere, anywhere],
-        out_specs=(anywhere,) * 2,
+        out_specs=anywhere,
         scratch_shapes=[vmem((SLOTS + 7, GROUP, 512), jnp.bfloat16)] * 4
         + [vmem((Q_ROWS, 256), jnp.bfloat16)]
-        + [vmem((3 * QB, 128), jnp.bfloat16)] * 2
+        + [vmem((3 * QB, 256), jnp.bfloat16)]
         + [vmem((3 * QB, 128), jnp.float32)] * 2
         + [vmem((3 * QB, 256), jnp.float32)] * 2
         + [dma(shape) for shape in sems]
-        + [dma, dma],
+        + [dma],
         compiler_params=pltpu.CompilerParams(
             collective_id=0, has_side_effects=True, vmem_limit_bytes=62 * 2**20
         ),
@@ -583,7 +565,10 @@
 
 def on_device(queries, keys, values, d_queries, d_keys, d_values, positions, key_lists):
     pkv, pq, table = rotate_all(queries, keys, values, d_queries, d_keys, d_values, positions, key_lists)
-    return bring_attend_return(table, pkv, pq)
+    by_head = bring_attend_return(table, pkv, pq)
+    return tuple(
+        by_head[:, :, first : first + 128].transpose(1, 0, 2).reshape(CHUNK, 3072) for first in (0, 128)
+    )
 
 
 def solution(mesh):

time: 185 us -> 176 us (0.951)
  the two profiles are of different devices: /device:TPU:0 before, /device:TPU:50 now
where the time goes in v3:
time: 176 us
  Pallas kernels  169 us (96%)
  local copies, waits for them, and re-layouts  5.93 us (3%)
    pallas_call x1, Pallas kernels, bring_attend_return(): pl.pallas_call(whole_kernel, name='bring_attend_return', out_shape=jax.Sh...  161 us
    pallas_call x1, Pallas kernels, rotate_all(): pl.pallas_call(rotate_kernel, name='rotate', grid=(steps,), out_shape=(ja...  7.57 us
    unnamed x3, local copies, waits for them, and re-layouts  3.69 us

profile of v3, /device:TPU:50, one launch (start us, length us, event | category | flops | bytes accessed | tf_op | source)
XLA Modules:
  0.0 175.6 jit_solution(10378943755025961337)
XLA Ops:
  0.6 1.4 copy.13.lists_ref
  2.0 7.6 %rotate.1 = (bf16[24,128,512]{2,1,0:T(8,128)(2,1)}, bf16[24,128,256]{2,1,0:T(8,128)(2,1)}, s32[6,5]{1,0:T(8,128)}) custom-call(s32[16,5]{1,0:T(8,128)} %copy.13.lists_ref, s32[3,128]{1,0:T(4,128)} %spots_ref.1, f32[3,128]{1,0:T(4,128)} %constant.4.clone.rates_ref, bf16[128,128]{1,0:T(8,128)(2,1)} %constant.5.clone.swap_ref, bf16[128,3072]{1,0:T(8,128)(2,1)} %q_ref.1, ...), custom_call_target="tpu_custom_call" | custom-call | tf_op jit(solution)/shard_map/rotate/pallas_call | solution.py:143
  9.6 161.4 %bring_attend_return.1 = bf16[24,128,256]{2,1,0:T(8,128)(2,1)} custom-call(s32[6,5]{1,0:T(8,128)} %get-tuple-element.5.table, bf16[24,128,512]{2,1,0:T(8,128)(2,1)} %get-tuple-element.6.pkv, bf16[24,128,256]{2,1,0:T(8,128)(2,1)} %get-tuple-element.7.pq), custom_call_target="tpu_custom_call" | custom-call | tf_op jit(solution)/shard_map/bring_attend_return/pallas_call | solution.py:547
  171.0 1.5 slice_bitcast_fusion
  172.5 0.4 copy.15
  172.9 1.2 copy.17
  174.0 0.4 copy.14
  174.4 1.2 copy.16

commit v4 on v3

--- a/solution.py
+++ b/solution.py
@@ -533,7 +533,7 @@
     return first, between
 
 
-PROGRAM = make_program("01234abc", 3, 1, 3, 7, (1, 2, 3, 3))
+PROGRAM = make_program("0123a4bc", 3, 1, 3, 6, (1, 2, 3))
 
 
 def bring_attend_return(table, pkv, pq):

time: 176 us -> 173 us (0.983)
  the two profiles are of different devices: /device:TPU:50 before, /device:TPU:0 now
where the time goes in v4:
time: 173 us; the launch traced here: 170 us
  Pallas kernels  164 us (95%)
  local copies, waits for them, and re-layouts  5.93 us (3%)
    pallas_call x1, Pallas kernels, bring_attend_return(): pl.pallas_call(whole_kernel, name='bring_attend_return', out_shape=jax.Sh...  156 us
    pallas_call x1, Pallas kernels, rotate_all(): pl.pallas_call(rotate_kernel, name='rotate', grid=(steps,), out_shape=(ja...  7.57 us
    unnamed x3, local copies, waits for them, and re-layouts  3.69 us

profile of v4, /device:TPU:0, one launch (start us, length us, event | category | flops | bytes accessed | tf_op | source)
XLA Modules:
  0.0 170.2 jit_solution(16283684033983466132)
XLA Ops:
  0.6 1.4 copy.13.lists_ref
  2.0 7.6 %rotate.1 = (bf16[24,128,512]{2,1,0:T(8,128)(2,1)}, bf16[24,128,256]{2,1,0:T(8,128)(2,1)}, s32[6,5]{1,0:T(8,128)}) custom-call(s32[16,5]{1,0:T(8,128)} %copy.13.lists_ref, s32[3,128]{1,0:T(4,128)} %spots_ref.1, f32[3,128]{1,0:T(4,128)} %constant.4.clone.rates_ref, bf16[128,128]{1,0:T(8,128)(2,1)} %constant.5.clone.swap_ref, bf16[128,3072]{1,0:T(8,128)(2,1)} %q_ref.1, ...), custom_call_target="tpu_custom_call" | custom-call | tf_op jit(solution)/shard_map/rotate/pallas_call | solution.py:143
  9.6 156.0 %bring_attend_return.1 = bf16[24,128,256]{2,1,0:T(8,128)(2,1)} custom-call(s32[6,5]{1,0:T(8,128)} %get-tuple-element.5.table, bf16[24,128,512]{2,1,0:T(8,128)(2,1)} %get-tuple-element.6.pkv, bf16[24,128,256]{2,1,0:T(8,128)(2,1)} %get-tuple-element.7.pq), custom_call_target="tpu_custom_call" | custom-call | tf_op jit(solution)/shard_map/bring_attend_return/pallas_call | solution.py:547
  165.6 1.5 slice_bitcast_fusion
  167.1 0.4 copy.15
  167.5 1.2 copy.17
  168.6 0.4 copy.14
  169.0 1.2 copy.16
